TPU v7x, 32 devices: a whole 2x2x4 slice. The times are simulated.
32 devices in a mesh: tm: 16 (over z, x, core), space: 2 (over y).
Axes of the slice: x: 2, y: 2, z: 4, core: 2. Of those that a mesh axis runs over, the one named last changes fastest.
Arguments:
- state: bfloat16 [16, 32, 64, 128], P('tm', 'space'), may hold values from -4 to 4
- initial: bfloat16 [32, 64, 128], P('space'), may hold values from -4 to 4
- forcing: bfloat16 [16, 32, 64, 128], P('tm', 'space'), may hold values from -5 to 5
- kappa: bfloat16 [32, 64, 128], P('space'), may hold values from 0.5 to 2
- reaction: bfloat16 [32, 64, 128], P('space'), may hold values from 0.019897461 to 0.19921875
Outputs:
- updated: bfloat16 [16, 32, 64, 128], P('tm', 'space')
All inputs are finite; a program needn't handle non-finite values.
Results may differ from a plain program's by a relative error of at most 0.006.
The roundings to bfloat16 on the way count: a program that leaves them out, or rounds other values in their place, can miss the bound.
Values may be sent and summed in bfloat16 or wider, within the bound.
A program may use at most 64 MiB of HBM per device.

v0:
```python
import math

import jax
import jax.numpy as jnp
from jax import lax
from jax.sharding import PartitionSpec as P

SWEEPS = 6


alpha_ratio = 0.25
near_weight = 0.5
far_weight = 1.0
centre_weight = 6.0 * (near_weight + far_weight)
highest = lax.Precision.HIGHEST


def passed_along(value, axis, steps):
    count = lax.axis_size(axis)
    initial, last = (max(0, -steps), min(count, count - steps))
    return lax.ppermute(value, axis, [(source, source + steps) for source in range(initial, last)])


def with_halo(block, sides, width):
    for axis, dim in sides:
        count = lax.axis_size(axis)
        forward = [(i, i + 1) for i in range(count - 1)]
        backward = [(target, source) for source, target in forward]
        low = lax.ppermute(
            lax.slice_in_dim(block, block.shape[dim] - width, None, axis=dim), axis, forward
        )
        high = lax.ppermute(lax.slice_in_dim(block, 0, width, axis=dim), axis, backward)
        block = jnp.concatenate([low, block, high], axis=dim)
    return block


def shifted(values, axis_number, offset):
    extent = values.shape[axis_number]
    widths = [(0, 0)] * values.ndim
    widths[axis_number] = (2, 2)
    padded = jnp.pad(values, widths)
    return lax.slice_in_dim(padded, 2 + offset, 2 + offset + extent, axis=axis_number)


def stencil(source, offset, start, extent):
    axis_first = source.ndim - 3

    def planes_at(displacement):
        lower = offset + start + displacement
        return lax.slice_in_dim(source, lower, lower + extent, axis=axis_first)

    centre = planes_at(0)
    near_sum = planes_at(1) + planes_at(-1)
    far_sum = planes_at(2) + planes_at(-2)
    for axis_number in (axis_first + 1, axis_first + 2):
        near_sum = near_sum + shifted(centre, axis_number, 1) + shifted(centre, axis_number, -1)
        far_sum = far_sum + shifted(centre, axis_number, 2) + shifted(centre, axis_number, -2)
    return (centre, near_sum, far_sum)


def residual_of(centre, near_sum, far_sum, before, source_term, kappa_part, reaction_part):
    return (
        source_term
        - centre
        + before
        - kappa_part * (centre_weight * centre - near_weight * near_sum - far_weight * far_sum)
        - reaction_part * centre * centre * centre
    )


def tables(length):
    counter = jnp.arange(length, dtype=jnp.int32)
    product = counter[:, None] * counter[None, :] % length
    angles = product.astype(jnp.float32) * (2.0 * math.pi / length)
    scaling = jnp.exp(counter.astype(jnp.float32) * (math.log(alpha_ratio) / length))
    forward_cos = jnp.cos(angles) * scaling[None, :]
    forward_sin = -jnp.sin(angles) * scaling[None, :]
    unscale = 1.0 / (scaling * length)
    inverse_cos = jnp.cos(angles) * unscale[:, None]
    inverse_sin = -jnp.sin(angles) * unscale[:, None]
    return (forward_cos, forward_sin, inverse_cos, inverse_sin)


def mode_shift(index_values, length):
    phases = index_values * (2.0 * math.pi / length)
    factor = math.exp(math.log(alpha_ratio) / length)
    return (1.0 - factor * jnp.cos(phases), factor * jnp.sin(phases))


def sweep_weights():
    return [
        1.0 / (1.0 + 0.4 * math.cos(math.pi * (2 * rounds + 1) / (2 * SWEEPS)))
        for rounds in range(SWEEPS)
    ]


def divided(error_real, error_imag, base_part, shift_real, shift_imag):
    diag_real = shift_real + base_part
    magnitude = diag_real * diag_real + shift_imag * shift_imag
    return jnp.stack(
        [
            (error_real * diag_real + error_imag * shift_imag) / magnitude,
            (error_imag * diag_real - error_real * shift_imag) / magnitude,
        ]
    )


def update(
    centre, near_sum, far_sum, target, kappa_part, base_part, shift_real, shift_imag, weight
):
    applied = base_part * centre - kappa_part * (near_weight * near_sum + far_weight * far_sum)
    image_real = shift_real * centre[0] - shift_imag * centre[1] + applied[0]
    image_imag = shift_real * centre[1] + shift_imag * centre[0] + applied[1]
    error_real = target[0] - image_real
    error_imag = target[1] - image_imag
    return centre + weight * divided(error_real, error_imag, base_part, shift_real, shift_imag)


def on_device(state, initial, forcing, kappa, reaction):
    local_steps, width_x, rows_y, depth_z = state.shape
    members = lax.axis_size("tm")
    length = local_steps * members
    position = lax.axis_index("tm")
    slab_index = lax.axis_index("space")
    columns = rows_y * depth_z
    kappa_full = kappa.astype(jnp.float32)
    reaction_full = reaction.astype(jnp.float32)
    start_state = initial.astype(jnp.float32)
    before = passed_along(state[local_steps - 1], "tm", 1)
    opening = jnp.where(position == 0, initial, before)
    previous = jnp.concatenate([opening[None], state[:-1]], axis=0)
    forward_cos, forward_sin, inverse_cos, inverse_sin = tables(length)
    padded = with_halo(state, (("space", 1),), 2)
    residual_centre, residual_near_sum, residual_far_sum = stencil(
        padded.astype(jnp.float32), 2, 0, width_x
    )
    result = residual_of(
        residual_centre,
        residual_near_sum,
        residual_far_sum,
        previous.astype(jnp.float32),
        forcing.astype(jnp.float32),
        kappa_full,
        reaction_full,
    )
    residual = result.astype(jnp.bfloat16).reshape(local_steps, width_x, columns)
    cells = lax.all_to_all(residual, "tm", split_axis=2, concat_axis=0, tiled=True)
    share = cells.shape[2]
    flat_cells = cells.reshape(length, width_x * share).astype(jnp.float32)
    spectrum = jnp.stack(
        [
            jnp.dot(forward_cos, flat_cells, precision=highest),
            jnp.dot(forward_sin, flat_cells, precision=highest),
        ]
    )
    spectrum = spectrum.astype(jnp.bfloat16).reshape(2, length, width_x, share)
    modes = lax.all_to_all(spectrum, "tm", split_axis=1, concat_axis=3, tiled=True)
    target = modes.astype(jnp.float32).reshape(2, local_steps, width_x, rows_y, depth_z)
    index_values = (position * local_steps + jnp.arange(local_steps, dtype=jnp.int32)).astype(
        jnp.float32
    )
    shift_real, shift_imag = mode_shift(index_values, length)
    shift_real = shift_real.reshape(local_steps, 1, 1, 1)
    shift_imag = shift_imag.reshape(local_steps, 1, 1, 1)
    sigma_rate = 3.0 * reaction_full * start_state * start_state
    base_rate = kappa_full * centre_weight + sigma_rate
    weights = sweep_weights()
    iterate = divided(target[0], target[1], base_rate, shift_real, shift_imag)
    stacked = jnp.concatenate(
        [
            target.reshape(2 * local_steps, width_x, rows_y, depth_z),
            kappa_full[None],
            sigma_rate[None],
        ],
        axis=0,
    )
    rim_data = with_halo(stacked, (("space", 1),), 2)
    wide_target = rim_data[: 2 * local_steps].reshape(2, local_steps, width_x + 4, rows_y, depth_z)
    wide_kappa = rim_data[2 * local_steps]
    wide_base = wide_kappa * centre_weight + rim_data[2 * local_steps + 1]
    global_x = slab_index * width_x + jnp.arange(width_x + 4, dtype=jnp.int32) - 2
    inside_mask = ((global_x >= 0) & (global_x < width_x * lax.axis_size("space"))).astype(
        jnp.float32
    )
    inside_mask = inside_mask[:, None, None]
    for pair_index in range(len(weights) // 2):
        padded_iterate = with_halo(iterate, (("space", 2),), 4)
        centre, near_sum, far_sum = stencil(padded_iterate, 4, -2, width_x + 4)
        widened = (
            update(
                centre,
                near_sum,
                far_sum,
                wide_target,
                wide_kappa,
                wide_base,
                shift_real,
                shift_imag,
                weights[2 * pair_index],
            )
            * inside_mask
        )
        centre, near_sum, far_sum = stencil(widened, 2, 0, width_x)
        iterate = update(
            centre,
            near_sum,
            far_sum,
            target,
            kappa_full,
            base_rate,
            shift_real,
            shift_imag,
            weights[2 * pair_index + 1],
        )
    solved = iterate.astype(jnp.bfloat16).reshape(2, local_steps, width_x, columns)
    gathered = lax.all_to_all(solved, "tm", split_axis=3, concat_axis=1, tiled=True)
    real_part = gathered[0].reshape(length, width_x * share).astype(jnp.float32)
    imag_part = gathered[1].reshape(length, width_x * share).astype(jnp.float32)
    correction = (
        jnp.dot(inverse_cos, real_part, precision=highest)
        + jnp.dot(inverse_sin, imag_part, precision=highest)
    ).astype(jnp.bfloat16)
    correction = correction.reshape(length, width_x, share)
    returned = lax.all_to_all(correction, "tm", split_axis=0, concat_axis=2, tiled=True)
    return (state.astype(jnp.float32) + returned.reshape(state.shape).astype(jnp.float32)).astype(
        jnp.bfloat16
    )


def solution(mesh):
    placed = (
        P("tm", "space", None, None),
        P("space", None, None),
        P("tm", "space", None, None),
        P("space", None, None),
        P("space", None, None),
    )
    return jax.shard_map(
        on_device,
        mesh=mesh,
        in_specs=placed,
        out_specs=P("tm", "space", None, None),
        check_vma=False,
    )
```

profile of v0, /device:TPU:0, one launch (start us, length us, event | category | flops | bytes accessed | tf_op | source)
XLA Modules:
  0.0 237.0 jit_solution(5456175213582272566)
XLA Ops:
  0.0 2.5 %collective-permute-start.2 = (bf16[16,64,128]{2,1,0:T(8,128)(2,1)}, bf16[16,64,128]{2,1,0:T(8,128)(2,1)S(1)}, u32[]{:S(2)}, u32[]{:S(2)}) collective-permute-start(bf16[16,64,128]{2,1,0:T(8,128)(2,1)} %bitcast.223), channel_id=1, source_target_pairs={{0,2},{2,4},{4,6},{6,8},{8,10},{10,12},{12,14},{14,16},{16,18},{18... | collective-permute-start | bytes 786440 | tf_op jit(solution)/shard_map/ppermute | solution.py:21
  2.5 0.8 fusion.184
  3.3 4.2 %collective-permute-start = (bf16[1,2,64,128]{3,2,1,0:T(8,128)(2,1)S(1)}, bf16[1,2,64,128]{3,2,1,0:T(8,128)(2,1)S(1)}, u32[]{:S(2)}, u32[]{:S(2)}) collective-permute-start(bf16[1,2,64,128]{3,2,1,0:T(8,128)(2,1)S(1)} %get-tuple-element.41), channel_id=1, source_target_pairs={{0,1},{2,3},{4,5},{6,7},{8,9},{10,11},{12,13},{14,15},{16,17},{18,... | collective-permute-start | bytes 98312 | tf_op jit(solution)/shard_map/ppermute | solution.py:29
  7.6 1.3 collective-permute-start.1
  9.2 4.2 %collective-permute-done.1 = bf16[1,2,64,128]{3,2,1,0:T(8,128)(2,1)S(1)} collective-permute-done((bf16[1,2,64,128]{3,2,1,0:T(8,128)(2,1)S(1)}, bf16[1,2,64,128]{3,2,1,0:T(8,128)(2,1)S(1)}, u32[]{:S(2)}, u32[]{:S(2)}) %collective-permute-start.1) | collective-permute-done | bytes 32800 | tf_op jit(solution)/shard_map/ppermute | solution.py:32
  13.4 1.0 maximum_convert_fusion
  14.5 0.8 fusion.107
  15.4 6.7 %copy.27 = bf16[1,16,8192]{1,0,2:T(2,128)(2,1)} copy(bf16[1,16,8192]{2,1,0:T(8,128)(2,1)S(1)} %reshape.976) | data formatting | bytes 524288 | tf_op jit(solution)/shard_map/reshape | solution.py:146
  22.1 0.5 broadcast.386
  22.7 45.2 %reduce = bf16[8192,16]{1,0:T(8,128)(2,1)S(1)} reduce(bf16[8192,1,16]{2,1,0:T(2,128)(2,1)} %bitcast.218, bf16[]{:T(256)} %broadcast.386), dimensions={1}, to_apply=%bitcast.165.reduce_sub_computation | reduce | bytes 524290
  67.9 2.8 %reshape.994 = bf16[16,2,4096]{2,1,0:T(2,128)(2,1)} reshape(bf16[8192,16]{1,0:T(8,128)(2,1)S(1)} %reduce) | data formatting | bytes 524288
  70.7 6.1 %all-to-all-start = ((bf16[16,2,4096]{2,1,0:T(2,128)(2,1)}), bf16[16,2,4096]{2,1,0:T(2,128)(2,1)S(1)}, u32[]{:S(2)}, u32[]{:S(2)}) async-start(bf16[16,2,4096]{2,1,0:T(2,128)(2,1)} %reshape.994), calls=%async_computation | async-start | bytes 524288 | tf_op jit(solution)/shard_map/all_to_all | solution.py:147
  76.8 10.0 %all-to-all-done = bf16[16,2,4096]{2,1,0:T(2,128)(2,1)S(1)} async-done(((bf16[16,2,4096]{2,1,0:T(2,128)(2,1)}), bf16[16,2,4096]{2,1,0:T(2,128)(2,1)S(1)}, u32[]{:S(2)}, u32[]{:S(2)}) %all-to-all-start) | async-done | bytes 262176 | tf_op jit(solution)/shard_map/all_to_all | solution.py:147
  86.8 7.6 %reshape.995 = bf16[8192,1,16]{2,1,0:T(2,128)(2,1)} reshape(bf16[16,2,4096]{2,1,0:T(2,128)(2,1)S(1)} %all-to-all-done) | data formatting | bytes 524288
  94.4 7.9 %copy.28 = bf16[1,16,8192]{2,1,0:T(8,128)(2,1)S(1)} copy(bf16[1,16,8192]{1,0,2:T(2,128)(2,1)} %bitcast.219) | data formatting | bytes 524288 | tf_op jit(solution)/shard_map/all_to_all | solution.py:147
  102.4 0.4 fusion.43
  102.8 0.4 fusion.44
  103.3 1.1 copy.32
  104.4 3.8 %all-to-all-start.1 = ((bf16[2,16,16,512]{3,2,0,1:T(8,128)(2,1)}), bf16[2,16,16,512]{3,2,0,1:T(8,128)(2,1)S(1)}, u32[]{:S(2)}, u32[]{:S(2)}) async-start(bf16[2,16,16,512]{3,2,0,1:T(8,128)(2,1)} %copy.32), calls=%async_computation.1 | async-start | bytes 1048576 | tf_op jit(solution)/shard_map/all_to_all | solution.py:157
  108.4 13.9 %all-to-all-done.1 = bf16[2,16,16,512]{3,2,0,1:T(8,128)(2,1)S(1)} async-done(((bf16[2,16,16,512]{3,2,0,1:T(8,128)(2,1)}), bf16[2,16,16,512]{3,2,0,1:T(8,128)(2,1)S(1)}, u32[]{:S(2)}, u32[]{:S(2)}) %all-to-all-start.1) | async-done | bytes 524320 | tf_op jit(solution)/shard_map/all_to_all | solution.py:157
  122.6 1.6 copy.35
  124.2 0.3 copy.33
  124.5 0.3 copy.34
  124.9 1.3 reshape.985
  126.2 1.3 divide_bitcast_fusion.13
  127.6 1.6 collective-permute-start.5
  129.2 1.3 collective-permute-start.6
  130.7 4.6 %collective-permute-start.3 = (f32[2,1,4,64,128]{4,3,2,1,0:T(8,128)S(1)}, f32[2,1,4,64,128]{4,3,2,1,0:T(8,128)S(1)}, u32[]{:S(2)}, u32[]{:S(2)}) collective-permute-start(f32[2,1,4,64,128]{4,3,2,1,0:T(8,128)S(1)} %get-tuple-element.32), channel_id=1, source_target_pairs={{0,1},{2,3},{4,5},{6,7},{8,9},{10,11},{12,13},{14,15},{16,17},{18,... | collective-permute-start | bytes 786440 | tf_op jit(solution)/shard_map/ppermute | solution.py:29
  135.3 1.3 collective-permute-start.4
  136.6 2.4 %collective-permute-done.6 = f32[4,2,64,128]{3,2,1,0:T(8,128)S(1)} collective-permute-done((f32[4,2,64,128]{3,2,1,0:T(8,128)S(1)}, f32[4,2,64,128]{3,2,1,0:T(8,128)S(1)}, u32[]{:S(2)}, u32[]{:S(2)}) %collective-permute-start.6) | collective-permute-done | bytes 262176 | tf_op jit(solution)/shard_map/ppermute | solution.py:32
  139.5 1.0 collective-permute-done.3
  140.5 4.1 %collective-permute-done.4 = f32[2,1,4,64,128]{4,3,2,1,0:T(8,128)S(1)} collective-permute-done((f32[2,1,4,64,128]{4,3,2,1,0:T(8,128)S(1)}, f32[2,1,4,64,128]{4,3,2,1,0:T(8,128)S(1)}, u32[]{:S(2)}, u32[]{:S(2)}) %collective-permute-start.4) | collective-permute-done | bytes 262176 | tf_op jit(solution)/shard_map/ppermute | solution.py:32
  145.0 1.8 fusion.8
  146.8 0.6 divide_bitcast_fusion.5
  148.0 1.2 fusion.52
  149.2 0.4 divide_bitcast_fusion.11
  150.0 1.5 collective-permute-start.7
  151.5 1.3 collective-permute-start.8
  152.8 2.8 %collective-permute-done.7 = f32[2,1,4,64,128]{4,3,2,1,0:T(8,128)S(1)} collective-permute-done((f32[2,1,4,64,128]{4,3,2,1,0:T(8,128)S(1)}, f32[2,1,4,64,128]{4,3,2,1,0:T(8,128)S(1)}, u32[]{:S(2)}, u32[]{:S(2)}) %collective-permute-start.7) | collective-permute-done | bytes 262176 | tf_op jit(solution)/shard_map/ppermute | solution.py:29
  155.6 4.1 %collective-permute-done.8 = f32[2,1,4,64,128]{4,3,2,1,0:T(8,128)S(1)} collective-permute-done((f32[2,1,4,64,128]{4,3,2,1,0:T(8,128)S(1)}, f32[2,1,4,64,128]{4,3,2,1,0:T(8,128)S(1)}, u32[]{:S(2)}, u32[]{:S(2)}) %collective-permute-start.8) | collective-permute-done | bytes 262176 | tf_op jit(solution)/shard_map/ppermute | solution.py:32
  160.1 1.8 fusion.20
  161.8 0.6 divide_bitcast_fusion.3
  162.9 1.2 fusion.64
  164.1 0.4 divide_bitcast_fusion.9
  165.0 1.3 collective-permute-start.10
  166.3 4.8 %collective-permute-start.9 = (f32[2,1,4,64,128]{4,3,2,1,0:T(8,128)S(1)}, f32[2,1,4,64,128]{4,3,2,1,0:T(8,128)S(1)}, u32[]{:S(2)}, u32[]{:S(2)}) collective-permute-start(f32[2,1,4,64,128]{4,3,2,1,0:T(8,128)S(1)} %get-tuple-element.28), channel_id=1, source_target_pairs={{0,1},{2,3},{4,5},{6,7},{8,9},{10,11},{12,13},{14,15},{16,17},{18,... | collective-permute-start | bytes 786440 | tf_op jit(solution)/shard_map/ppermute | solution.py:29
  171.1 2.2 collective-permute-done.10
  173.2 1.5 collective-permute-done.9
  175.0 1.8 fusion.32
  176.8 0.6 divide_bitcast_fusion.1
  177.9 1.2 fusion.76
  179.1 0.4 divide_bitcast_fusion.7
  179.9 4.7 %copy.41 = bf16[2,1,16,64,128]{2,0,4,3,1:T(2,128)(2,1)} copy(bf16[2,1,16,64,128]{4,3,2,1,0:T(8,128)(2,1)S(1)} %fusion.84) | data formatting | bytes 1048576 | tf_op jit(solution)/shard_map/reshape | solution.py:215
  184.6 6.4 %reshape.996 = bf16[16,2,8192]{2,1,0:T(2,128)(2,1)} reshape(bf16[8192,1,2,16]{3,2,1,0:T(2,128)(2,1)} %bitcast.216) | data formatting | bytes 1048576
  191.0 4.6 %all-to-all-start.2 = ((bf16[16,2,8192]{2,1,0:T(2,128)(2,1)}), bf16[16,2,8192]{2,1,0:T(2,128)(2,1)S(1)}, u32[]{:S(2)}, u32[]{:S(2)}) async-start(bf16[16,2,8192]{2,1,0:T(2,128)(2,1)} %reshape.996), calls=%async_computation.2 | async-start | bytes 1048576 | tf_op jit(solution)/shard_map/all_to_all | solution.py:216
  195.6 14.5 %all-to-all-done.2 = bf16[16,2,8192]{2,1,0:T(2,128)(2,1)S(1)} async-done(((bf16[16,2,8192]{2,1,0:T(2,128)(2,1)}), bf16[16,2,8192]{2,1,0:T(2,128)(2,1)S(1)}, u32[]{:S(2)}, u32[]{:S(2)}) %all-to-all-start.2) | async-done | bytes 524320 | tf_op jit(solution)/shard_map/all_to_all | solution.py:216
  210.1 4.1 %reshape.997 = bf16[8192,1,2,16]{3,2,1,0:T(2,128)(2,1)} reshape(bf16[16,2,8192]{2,1,0:T(2,128)(2,1)S(1)} %all-to-all-done.2) | data formatting | bytes 1048576
  214.2 6.1 %copy.42 = bf16[2,1,16,16,512]{4,3,2,0,1:T(8,128)(2,1)S(1)} copy(bf16[2,1,16,16,512]{2,0,4,3,1:T(2,128)(2,1)} %bitcast.217) | data formatting | bytes 1048576 | tf_op jit(solution)/shard_map/all_to_all | solution.py:216
  220.4 0.4 fusion.137
  220.8 0.4 fusion
  221.3 13.9 %all_to_all.48 = bf16[16,16,512]{2,1,0:T(8,128)(2,1)S(1)} all-to-all(bf16[16,16,512]{2,1,0:T(8,128)(2,1)S(1)} %bitcast.225), channel_id=1, replica_groups=mesh['tm'=16,'space'=2] {'tm'}, dimensions={0} | all-to-all | bytes 524288 | tf_op jit(solution)/shard_map/all_to_all | solution.py:224
  235.3 0.3 copy.40
  235.7 0.5 copy-done.1
  236.2 0.8 add_convert_fusion
  (59 shorter events, 5.5 us)
Async XLA Ops:
  0.0 14.4 %copy-start.3 = (bf16[16,64,128]{2,1,0:T(8,128)(2,1)S(1)}, bf16[16,64,128]{2,1,0:T(8,128)(2,1)}, u32[]{:S(2)}) copy-start(bf16[16,64,128]{2,1,0:T(8,128)(2,1)} %param.6) | copy-start | bytes 786436
  0.0 14.5 %copy-start.4 = (bf16[1,16,64,128]{3,2,1,0:T(8,128)(2,1)S(1)}, bf16[1,16,64,128]{3,2,1,0:T(8,128)(2,1)}, u32[]{:S(2)}) copy-start(bf16[1,16,64,128]{3,2,1,0:T(8,128)(2,1)} %param.7) | copy-start | bytes 786436
  0.0 14.5 %copy-start = (bf16[16,64,128]{2,1,0:T(8,128)(2,1)S(1)}, bf16[16,64,128]{2,1,0:T(8,128)(2,1)}, u32[]{:S(2)}) copy-start(bf16[16,64,128]{2,1,0:T(8,128)(2,1)} %param.8) | copy-start | bytes 786436
  0.0 14.5 %copy-start.2 = (bf16[16,64,128]{2,1,0:T(8,128)(2,1)S(1)}, bf16[16,64,128]{2,1,0:T(8,128)(2,1)}, u32[]{:S(2)}) copy-start(bf16[16,64,128]{2,1,0:T(8,128)(2,1)} %param.9) | copy-start | bytes 786436
  0.0 14.4 %collective-permute-start.2 = (bf16[16,64,128]{2,1,0:T(8,128)(2,1)}, bf16[16,64,128]{2,1,0:T(8,128)(2,1)S(1)}, u32[]{:S(2)}, u32[]{:S(2)}) collective-permute-start(bf16[16,64,128]{2,1,0:T(8,128)(2,1)} %bitcast.223), channel_id=1, source_target_pairs={{0,2},{2,4},{4,6},{6,8},{8,10},{10,12},{12,14},{14,16},{16,18},{18... | collective-permute-start | bytes 786440 | tf_op jit(solution)/shard_map/ppermute | solution.py:21
  3.3 5.8 %collective-permute-start = (bf16[1,2,64,128]{3,2,1,0:T(8,128)(2,1)S(1)}, bf16[1,2,64,128]{3,2,1,0:T(8,128)(2,1)S(1)}, u32[]{:S(2)}, u32[]{:S(2)}) collective-permute-start(bf16[1,2,64,128]{3,2,1,0:T(8,128)(2,1)S(1)} %get-tuple-element.41), channel_id=1, source_target_pairs={{0,1},{2,3},{4,5},{6,7},{8,9},{10,11},{12,13},{14,15},{16,17},{18,... | collective-permute-start | bytes 98312 | tf_op jit(solution)/shard_map/ppermute | solution.py:29
  7.6 5.8 %collective-permute-start.1 = (bf16[1,2,64,128]{3,2,1,0:T(8,128)(2,1)S(1)}, bf16[1,2,64,128]{3,2,1,0:T(8,128)(2,1)S(1)}, u32[]{:S(2)}, u32[]{:S(2)}) collective-permute-start(bf16[1,2,64,128]{3,2,1,0:T(8,128)(2,1)S(1)} %get-tuple-element.42), channel_id=1, source_target_pairs={{1,0},{3,2},{5,4},{7,6},{9,8},{11,10},{13,12},{15,14},{17,16},{19,... | collective-permute-start | bytes 98312 | tf_op jit(solution)/shard_map/ppermute | solution.py:32
  70.7 16.1 %all-to-all-start = ((bf16[16,2,4096]{2,1,0:T(2,128)(2,1)}), bf16[16,2,4096]{2,1,0:T(2,128)(2,1)S(1)}, u32[]{:S(2)}, u32[]{:S(2)}) async-start(bf16[16,2,4096]{2,1,0:T(2,128)(2,1)} %reshape.994), calls=%async_computation | async-start | bytes 524288 | tf_op jit(solution)/shard_map/all_to_all | solution.py:147
  104.4 18.0 %all-to-all-start.1 = ((bf16[2,16,16,512]{3,2,0,1:T(8,128)(2,1)}), bf16[2,16,16,512]{3,2,0,1:T(8,128)(2,1)S(1)}, u32[]{:S(2)}, u32[]{:S(2)}) async-start(bf16[2,16,16,512]{3,2,0,1:T(8,128)(2,1)} %copy.32), calls=%async_computation.1 | async-start | bytes 1048576 | tf_op jit(solution)/shard_map/all_to_all | solution.py:157
  127.6 9.0 %collective-permute-start.5 = (f32[4,2,64,128]{3,2,1,0:T(8,128)S(1)}, f32[4,2,64,128]{3,2,1,0:T(8,128)S(1)}, u32[]{:S(2)}, u32[]{:S(2)}) collective-permute-start(f32[4,2,64,128]{3,2,1,0:T(8,128)S(1)} %get-tuple-element.26), channel_id=1, source_target_pairs={{0,1},{2,3},{4,5},{6,7},{8,9},{10,11},{12,13},{14,15},{16,17},{18,... | collective-permute-start | bytes 786440 | tf_op jit(solution)/shard_map/ppermute | solution.py:29
  129.2 9.8 %collective-permute-start.6 = (f32[4,2,64,128]{3,2,1,0:T(8,128)S(1)}, f32[4,2,64,128]{3,2,1,0:T(8,128)S(1)}, u32[]{:S(2)}, u32[]{:S(2)}) collective-permute-start(f32[4,2,64,128]{3,2,1,0:T(8,128)S(1)} %get-tuple-element.27), channel_id=1, source_target_pairs={{1,0},{3,2},{5,4},{7,6},{9,8},{11,10},{13,12},{15,14},{17,16},{19,... | collective-permute-start | bytes 786440 | tf_op jit(solution)/shard_map/ppermute | solution.py:32
  130.7 9.8 %collective-permute-start.3 = (f32[2,1,4,64,128]{4,3,2,1,0:T(8,128)S(1)}, f32[2,1,4,64,128]{4,3,2,1,0:T(8,128)S(1)}, u32[]{:S(2)}, u32[]{:S(2)}) collective-permute-start(f32[2,1,4,64,128]{4,3,2,1,0:T(8,128)S(1)} %get-tuple-element.32), channel_id=1, source_target_pairs={{0,1},{2,3},{4,5},{6,7},{8,9},{10,11},{12,13},{14,15},{16,17},{18,... | collective-permute-start | bytes 786440 | tf_op jit(solution)/shard_map/ppermute | solution.py:29
  135.3 9.4 %collective-permute-start.4 = (f32[2,1,4,64,128]{4,3,2,1,0:T(8,128)S(1)}, f32[2,1,4,64,128]{4,3,2,1,0:T(8,128)S(1)}, u32[]{:S(2)}, u32[]{:S(2)}) collective-permute-start(f32[2,1,4,64,128]{4,3,2,1,0:T(8,128)S(1)} %get-tuple-element.33), channel_id=1, source_target_pairs={{1,0},{3,2},{5,4},{7,6},{9,8},{11,10},{13,12},{15,14},{17,16},{19,... | collective-permute-start | bytes 786440 | tf_op jit(solution)/shard_map/ppermute | solution.py:32
  150.0 5.6 %collective-permute-start.7 = (f32[2,1,4,64,128]{4,3,2,1,0:T(8,128)S(1)}, f32[2,1,4,64,128]{4,3,2,1,0:T(8,128)S(1)}, u32[]{:S(2)}, u32[]{:S(2)}) collective-permute-start(f32[2,1,4,64,128]{4,3,2,1,0:T(8,128)S(1)} %get-tuple-element.30), channel_id=1, source_target_pairs={{0,1},{2,3},{4,5},{6,7},{8,9},{10,11},{12,13},{14,15},{16,17},{18,... | collective-permute-start | bytes 786440 | tf_op jit(solution)/shard_map/ppermute | solution.py:29
  151.5 8.3 %collective-permute-start.8 = (f32[2,1,4,64,128]{4,3,2,1,0:T(8,128)S(1)}, f32[2,1,4,64,128]{4,3,2,1,0:T(8,128)S(1)}, u32[]{:S(2)}, u32[]{:S(2)}) collective-permute-start(f32[2,1,4,64,128]{4,3,2,1,0:T(8,128)S(1)} %get-tuple-element.31), channel_id=1, source_target_pairs={{1,0},{3,2},{5,4},{7,6},{9,8},{11,10},{13,12},{15,14},{17,16},{19,... | collective-permute-start | bytes 786440 | tf_op jit(solution)/shard_map/ppermute | solution.py:32
  165.0 8.3 %collective-permute-start.10 = (f32[2,1,4,64,128]{4,3,2,1,0:T(8,128)S(1)}, f32[2,1,4,64,128]{4,3,2,1,0:T(8,128)S(1)}, u32[]{:S(2)}, u32[]{:S(2)}) collective-permute-start(f32[2,1,4,64,128]{4,3,2,1,0:T(8,128)S(1)} %get-tuple-element.29), channel_id=1, source_target_pairs={{1,0},{3,2},{5,4},{7,6},{9,8},{11,10},{13,12},{15,14},{17,16},{19,... | collective-permute-start | bytes 786440 | tf_op jit(solution)/shard_map/ppermute | solution.py:32
  166.3 8.4 %collective-permute-start.9 = (f32[2,1,4,64,128]{4,3,2,1,0:T(8,128)S(1)}, f32[2,1,4,64,128]{4,3,2,1,0:T(8,128)S(1)}, u32[]{:S(2)}, u32[]{:S(2)}) collective-permute-start(f32[2,1,4,64,128]{4,3,2,1,0:T(8,128)S(1)} %get-tuple-element.28), channel_id=1, source_target_pairs={{0,1},{2,3},{4,5},{6,7},{8,9},{10,11},{12,13},{14,15},{16,17},{18,... | collective-permute-start | bytes 786440 | tf_op jit(solution)/shard_map/ppermute | solution.py:29
  191.0 19.0 %all-to-all-start.2 = ((bf16[16,2,8192]{2,1,0:T(2,128)(2,1)}), bf16[16,2,8192]{2,1,0:T(2,128)(2,1)S(1)}, u32[]{:S(2)}, u32[]{:S(2)}) async-start(bf16[16,2,8192]{2,1,0:T(2,128)(2,1)} %reshape.996), calls=%async_computation.2 | async-start | bytes 1048576 | tf_op jit(solution)/shard_map/all_to_all | solution.py:216
  235.2 1.0 copy-start.1
where the time goes:
time: 238 us; the launch traced here: 237 us
  other arithmetic  64.9 us (27%)
  waiting for transfers between devices  61.1 us (26%)
  local copies, waits for them, and re-layouts  54.5 us (23%)
  starting transfers between devices  40.1 us (17%)
  blocking collectives  13.9 us (6%)
    unnamed x1, other arithmetic  45.2 us
    unnamed x19, local copies, waits for them, and re-layouts  22.2 us
    ppermute x5, waiting for transfers between devices, with_halo(): lax.ppermute(lax.slice_in_dim(block, 0, width, axis=dim), axis, backward)  17.1 us
    ppermute x5, starting transfers between devices, with_halo(): lax.ppermute(lax.slice_in_dim(block, block.shape[dim] - width, None, axis...  16.7 us
    all_to_all x1, waiting for transfers between devices, on_device(): lax.all_to_all(solved, 'tm', split_axis=3, concat_axis=1, tiled=True)  14.5 us
    all_to_all x1, blocking collectives, on_device(): lax.all_to_all(correction, 'tm', split_axis=0, concat_axis=2, tiled=True)  13.9 us
    all_to_all x1, waiting for transfers between devices, on_device(): lax.all_to_all(spectrum, 'tm', split_axis=1, concat_axis=3, tiled=True)  13.9 us
    all_to_all x1, waiting for transfers between devices, on_device(): lax.all_to_all(residual, 'tm', split_axis=2, concat_axis=0, tiled=True)  10 us
  transfers between devices with their start and end apart: 14, of which 12 were waited for; matrix products, arithmetic and copies ran while one was open for 1% of the time, Pallas kernels for 0%

commit v1 on v0

v1 whole, which is shorter than its diff:
```python
import functools
import math

import jax
import jax.numpy as jnp
from jax import lax
from jax.experimental import pallas as pl
from jax.experimental.pallas import tpu as pltpu
from jax.sharding import PartitionSpec as P

SWEEPS = 6
ALPHA = 0.25
MESH = pl.DeviceIdType.MESH
f32, bf16 = jnp.float32, jnp.bfloat16
REACH = 2 * SWEEPS


def sweep_weights():
    return [1.0 / (1.0 + 0.4 * math.cos(math.pi * (2 * k + 1) / (2 * SWEEPS))) for k in range(SWEEPS)]


def pick(index, values):
    out = jnp.float32(values[0])
    for k in range(1, len(values)):
        out = jnp.where(index == k, jnp.float32(values[k]), out)
    return out


def scaled_sum(terms):
    total = None
    for factor, value in terms:
        if abs(factor) < 1e-12:
            continue
        if abs(factor - 1.0) < 1e-12:
            total = value if total is None else total + value
        elif abs(factor + 1.0) < 1e-12:
            total = -value if total is None else total - value
        else:
            part = value * jnp.float32(factor)
            total = part if total is None else total + part
    return total


def forward_transform(values):
    n = len(values)
    h = n // 2
    s = [v * jnp.float32(ALPHA ** (k / n)) if k else v for k, v in enumerate(values)]
    even = {k: s[k] + s[n - k] for k in range(1, h)}
    odd = {k: s[k] - s[n - k] for k in range(1, h)}
    even[0], even[h] = s[0], s[h]
    out = [None] * h
    ang = 2.0 * math.pi / n
    re = [None] * (h + 1)
    im = [None] * (h + 1)
    for j in range(h // 2 + 1):
        a = scaled_sum([(math.cos(ang * ((j * k) % n)), even[k]) for k in range(0, h + 1, 2)])
        b = scaled_sum([(math.cos(ang * ((j * k) % n)), even[k]) for k in range(1, h + 1, 2)])
        re[j] = a if b is None else a + b
        if h - j != j:
            re[h - j] = a if b is None else a - b
        if j:
            c = scaled_sum([(math.sin(ang * ((j * k) % n)), odd[k]) for k in range(2, h, 2)])
            d = scaled_sum([(math.sin(ang * ((j * k) % n)), odd[k]) for k in range(1, h, 2)])
            if h - j != j:
                im[j] = -(c + d)
                im[h - j] = c - d
            else:
                parts = [v for v in (c, d) if v is not None]
                im[j] = -sum(parts[1:], parts[0])
    out[0] = (re[0], re[h])
    for j in range(1, h):
        out[j] = (re[j], im[j])
    return out


def inverse_transform(pairs):
    h = len(pairs)
    n = 2 * h
    ang = 2.0 * math.pi / n
    x0, xh = pairs[0]
    re = {j: pairs[j][0] for j in range(1, h)}
    im = {j: pairs[j][1] for j in range(1, h)}
    q = h // 2
    rp = {j: re[j] + re[h - j] for j in range(1, q)}
    rm = {j: re[j] - re[h - j] for j in range(1, q)}
    ip = {j: im[j] + im[h - j] for j in range(1, q)}
    im_ = {j: im[j] - im[h - j] for j in range(1, q)}
    out = [None] * n
    s, d = x0 + xh, x0 - xh
    for k in range(h + 1):
        cos = lambda j: 2.0 * math.cos(ang * ((j * k) % n))
        sin = lambda j: 2.0 * math.sin(ang * ((j * k) % n))
        r = rp if k % 2 == 0 else rm
        i = im_ if k % 2 == 0 else ip
        c_part = scaled_sum([(cos(j), r[j]) for j in range(1, q)] + [(cos(q), re[q])])
        s_part = scaled_sum([(sin(j), i[j]) for j in range(1, q)] + [(sin(q), im[q])])
        base = s if k % 2 == 0 else d
        total = base if c_part is None else base + c_part
        scale = lambda m: jnp.float32(1.0 / (ALPHA ** (m / n) * n))
        if s_part is None:
            out[k] = total * scale(k)
            if 0 < k < h:
                out[n - k] = total * scale(n - k)
        else:
            out[k] = (total - s_part) * scale(k)
            if 0 < k < h:
                out[n - k] = (total + s_part) * scale(n - k)
    return out


def lane_sum(x, lane):
    depth = x.shape[-1]
    zero = jnp.zeros_like(x)
    near = jnp.where(lane >= 1, pltpu.roll(x, 1, 1), zero) + jnp.where(
        lane < depth - 1, pltpu.roll(x, depth - 1, 1), zero
    )
    far = jnp.where(lane >= 2, pltpu.roll(x, 2, 1), zero) + jnp.where(
        lane < depth - 2, pltpu.roll(x, depth - 2, 1), zero
    )
    return near, far


def neighbour_sum(ref, p, row, size, lane):
    c = ref[p, row : row + size, :]
    near, far = lane_sum(c, lane)
    near = near + (ref[p - 1, row : row + size, :] + ref[p + 1, row : row + size, :])
    far = far + (ref[p - 2, row : row + size, :] + ref[p + 2, row : row + size, :])
    near = near + (ref[p, row - 1 : row - 1 + size, :] + ref[p, row + 1 : row + 1 + size, :])
    far = far + (ref[p, row - 2 : row - 2 + size, :] + ref[p, row + 2 : row + 2 + size, :])
    return c, near * 0.5 + far


def kernel(
    members, slabs, width, rows,
    state, initial, forcing, kappa, reaction, out,
    prev, halo, cext, res, buf1, spec, tgt, sol, buf3, corr, buf4,
    ca, cc, ci, x0r, x0i, ar, ai, br, bi,
    prev_s, prev_r, halo_s, halo_r, coef_s, coef_r, s1, r1, s2, r2, sg, rg, s3, r3, s4, r4,
):
    chips = members // 2
    half = width // 2
    hr = half * rows
    piece = hr // chips
    ext = half + 2 * REACH
    extra = REACH - half
    depth = state.shape[1]
    me = lax.axis_index("tm")
    slab = lax.axis_index("space")
    chip = lax.div(me, 2)
    core = lax.rem(me, 2)
    part = slab * 2 + core
    parts = 2 * slabs
    chunks = [(r, 16) for r in range(0, rows, 16)]

    barrier = pltpu.get_barrier_semaphore()

    def greet(k, _):
        other = lax.rem(me + k, members)
        pl.semaphore_signal(barrier, inc=1, device_id=(other, slab), device_id_type=MESH)
        return 0

    lax.fori_loop(1, members, greet, 0)
    has_low = slab > 0
    has_high = slab < slabs - 1
    for flag, step in ((has_low, -1), (has_high, 1)):
        @pl.when(flag)
        def _():
            for c in range(2):
                pl.semaphore_signal(
                    barrier, inc=1, device_id=(chip * 2 + c, slab + step), device_id_type=MESH
                )
    pl.semaphore_wait(
        barrier,
        members - 1 + 2 * has_low.astype(jnp.int32) + 2 * has_high.astype(jnp.int32),
    )

    def remote(src, dst, send, recv, device):
        return pltpu.make_async_remote_copy(
            src_ref=src, dst_ref=dst, send_sem=send, recv_sem=recv,
            device_id=device, device_id_type=MESH,
        )

    def prev_copy():
        return remote(state, prev, prev_s, prev_r, (lax.rem(me + 1, members), slab))

    @pl.when(me < members - 1)
    def _():
        prev_copy().start()

    def halo_copy(side):
        src = state.at[pl.ds((width - 2) * rows, 2 * rows), :] if side == 0 else state.at[pl.ds(0, 2 * rows), :]
        return remote(src, halo.at[side], halo_s.at[side], halo_r.at[side],
                      (me, slab + (1 if side == 0 else -1)))

    sends = (has_high, has_low)
    gets = (has_low, has_high)
    for side in range(2):
        @pl.when(sends[side])
        def _():
            halo_copy(side).start()

        @pl.when(jnp.logical_not(gets[side]))
        def _():
            halo[side] = jnp.zeros((2 * rows, depth), bf16)

    moves = (
        (1, 0, half, REACH - half),
        (-1, 0, half, REACH + half),
        (2, half - extra, extra, 0),
        (-2, 0, extra, REACH + 2 * half),
    )

    def there(step):
        return jnp.logical_and(part + step >= 0, part + step < parts)

    def device_at(step):
        target = part + step
        return (chip * 2 + lax.rem(target + 2, 2), lax.div(target + 2, 2) - 1)

    coefs = (kappa, reaction, initial)

    def coef_copy(m, a):
        step, first, count, place = moves[m]
        src = coefs[a].at[pl.ds(pl.multiple_of(core * hr + first * rows, 16), count * rows), :]
        return remote(src, cext.at[a, pl.ds(place * rows, count * rows), :],
                      coef_s.at[m, a], coef_r.at[m, a], device_at(step))

    def target_copy(m):
        step, first, count, place = moves[m]
        return remote(tgt.at[:, pl.ds((REACH + first) * rows, count * rows), :],
                      tgt.at[:, pl.ds(place * rows, count * rows), :],
                      sg.at[m], rg.at[m], device_at(step))

    for m, (step, first, count, place) in enumerate(moves):
        @pl.when(there(step))
        def _():
            for a in range(3):
                coef_copy(m, a).start()

        @pl.when(jnp.logical_not(there(-step)))
        def _():
            for a in range(3):
                cext[a, pl.ds(place * rows, count * rows), :] = jnp.zeros((count * rows, depth), bf16)
            for a in range(2):
                tgt[a, pl.ds(place * rows, count * rows), :] = jnp.zeros((count * rows, depth), bf16)

    for a in range(3):
        cext[a, pl.ds(REACH * rows, hr), :] = coefs[a][pl.ds(pl.multiple_of(core * hr, 16), hr), :]

    pad = jnp.zeros((8, depth), f32)

    def clear(p, _):
        for ref in (ar, ai, br, bi):
            ref[p, 0:8, :] = pad
            ref[p, 8 + rows : 16 + rows, :] = pad
        return 0

    lax.fori_loop(0, ext, clear, 0)
    lane = lax.broadcasted_iota(jnp.int32, (16, depth), 1)

    def widen(p, _):
        for r, n in chunks:
            at = pl.ds(pl.multiple_of(p * rows, 16) + r, n)
            ar[p + 2, 8 + r : 8 + r + n, :] = state[at, :].astype(f32)
        return 0

    lax.fori_loop(0, width, widen, 0)
    for side in range(2):
        @pl.when(gets[side])
        def _():
            halo_copy(side).wait_recv()
        for p in range(2):
            at = p if side == 0 else width + 2 + p
            ar[at, 8 : 8 + rows, :] = halo[side, p * rows : (p + 1) * rows, :].astype(f32)

    @pl.when(me == 0)
    def _():
        prev[...] = initial[...]

    @pl.when(me > 0)
    def _():
        prev_copy().wait_recv()

    def piece_copy(i):
        owner = 2 * lax.rem(i, chips) + lax.div(i, chips)
        return owner, remote(res.at[pl.ds(pl.multiple_of(i * piece, 16), piece), :], buf1.at[me],
                             s1.at[i], r1.at[me], (owner, slab))

    per_plane = rows // piece

    def residual_plane(k, _):
        p = lax.rem(k + core * half + lax.div(chip, per_plane) + 1, width)
        for r, n in chunks:
            at = pl.ds(pl.multiple_of(p * rows, 16) + r, n)
            c, total = neighbour_sum(ar, p + 2, 8 + r, n, lane)
            kap = kappa[at, :].astype(f32)
            value = (
                forcing[at, :].astype(f32) - c + prev[at, :].astype(f32)
                - kap * (9.0 * c - total)
                - reaction[at, :].astype(f32) * c * c * c
            )
            res[at, :] = value.astype(bf16)
        for sub in range(per_plane):
            i = p * per_plane + sub
            owner, copy = piece_copy(i)

            @pl.when(owner != me)
            def _():
                copy.start()
        return 0

    lax.fori_loop(0, width, residual_plane, 0)
    mine = core * chips + chip
    buf1[me] = res[pl.ds(pl.multiple_of(mine * piece, 16), piece), :]

    for m, (step, first, count, place) in enumerate(moves):
        @pl.when(there(-step))
        def _():
            for a in range(3):
                coef_copy(m, a).wait_recv()

    b = ALPHA ** (1.0 / members)
    ang = 2.0 * math.pi / members
    shift_a = pick(chip, [1.0 - b * math.cos(ang * j) for j in range(chips)])
    shift_c = pick(chip, [1.0 + b] + [1.0 - b * math.cos(ang * j) for j in range(1, chips)])
    shift_i = pick(chip, [0.0] + [b * math.sin(ang * j) for j in range(1, chips)])

    def coefficients(p, _):
        for r, n in chunks:
            at = pl.ds(pl.multiple_of(p * rows, 16) + r, n)
            kap = cext[0, at, :].astype(f32)
            ini = cext[2, at, :].astype(f32)
            base = 9.0 * kap + 3.0 * cext[1, at, :].astype(f32) * ini * ini
            da = shift_a + base
            dc = shift_c + base
            ia = 1.0 / (da * da + shift_i * shift_i)
            ic = 1.0 / (dc * dc + shift_i * shift_i)
            ca[at, :] = da * ia
            cc[at, :] = dc * ic
            ci[at, :] = shift_i * ia
        return 0

    lax.fori_loop(0, ext, coefficients, 0)

    def wait_1(n, _):
        @pl.when(n != me)
        def _():
            remote(res.at[pl.ds(0, piece), :], buf1.at[n], s1.at[0], r1.at[n], (me, slab)).wait_recv()
        return 0

    lax.fori_loop(0, members, wait_1, 0)

    def transform(t, _):
        at = pl.ds(pl.multiple_of(t * 16, 16), 16)
        pairs = forward_transform([buf1[n, at, :].astype(f32) for n in range(members)])
        for j in range(chips):
            spec[j, 0, at, :] = pairs[j][0].astype(bf16)
            spec[j, 1, at, :] = pairs[j][1].astype(bf16)
        return 0

    lax.fori_loop(0, piece // 16, transform, 0)

    def my_rows(first):
        return pl.ds(pl.multiple_of(first * rows + chip * piece, 16), piece)

    def spec_copy(j):
        return remote(spec.at[j], tgt.at[:, my_rows(REACH), :], s2.at[j], r2.at[chip],
                      (2 * j + core, slab))

    def send_2(k, _):
        spec_copy(lax.rem(chip + k, chips)).start()
        return 0

    lax.fori_loop(1, chips, send_2, 0)
    tgt[:, my_rows(REACH), :] = spec[chip]

    def wait_2(k, _):
        j = lax.rem(chip + k, chips)
        remote(spec.at[0], tgt.at[:, pl.ds(pl.multiple_of(REACH * rows + j * piece, 16), piece), :],
               s2.at[0], r2.at[j], (me, slab)).wait_recv()
        return 0

    lax.fori_loop(1, chips, wait_2, 0)
    for m, (step, first, count, place) in enumerate(moves):
        @pl.when(there(step))
        def _():
            target_copy(m).start()

    def opening(p, _):
        for r, n in chunks:
            at = pl.ds(pl.multiple_of(p * rows, 16) + r, n)
            yr = tgt[0, at, :].astype(f32)
            yi = tgt[1, at, :].astype(f32)
            kap = cext[0, at, :].astype(f32)
            a, c, i = ca[at, :], cc[at, :], ci[at, :]
            xr = yr * a + yi * i
            xi = yi * c - yr * i
            x0r[at, :] = xr
            x0i[at, :] = xi
            ar[p, 8 + r : 8 + r + n, :] = xr
            ai[p, 8 + r : 8 + r + n, :] = xi
            ca[at, :] = a * kap
            cc[at, :] = c * kap
            ci[at, :] = i * kap
        return 0

    lax.fori_loop(REACH, REACH + half, opening, 0)
    for m, (step, first, count, place) in enumerate(moves):
        @pl.when(there(-step))
        def _():
            target_copy(m).wait_recv()
    lax.fori_loop(0, REACH, opening, 0)
    lax.fori_loop(REACH + half, ext, opening, 0)

    weights = sweep_weights()
    for k in range(SWEEPS):
        sr, si, dr, di = (ar, ai, br, bi) if k % 2 == 0 else (br, bi, ar, ai)
        w = weights[k]
        last = k == SWEEPS - 1

        def sweep(p, _):
            for r, n in chunks:
                at = pl.ds(pl.multiple_of(p * rows, 16) + r, n)
                xr, tr = neighbour_sum(sr, p, 8 + r, n, lane)
                xi, ti = neighbour_sum(si, p, 8 + r, n, lane)
                i = ci[at, :]
                nr = (x0r[at, :] + ca[at, :] * tr + i * ti) * w + xr * (1.0 - w)
                ni = (x0i[at, :] + cc[at, :] * ti - i * tr) * w + xi * (1.0 - w)
                if last:
                    to = pl.ds(pl.multiple_of((p - REACH) * rows, 16) + r, n)
                    sol[0, to, :] = nr.astype(bf16)
                    sol[1, to, :] = ni.astype(bf16)
                else:
                    dr[p, 8 + r : 8 + r + n, :] = nr
                    di[p, 8 + r : 8 + r + n, :] = ni
            return 0

        lax.fori_loop(2 * k + 2, ext - 2 * k - 2, sweep, 0)

    def send_3(k, _):
        j = lax.rem(chip + k, chips)
        remote(sol.at[:, pl.ds(pl.multiple_of(j * piece, 16), piece), :], buf3.at[chip],
               s3.at[j], r3.at[chip], (2 * j + core, slab)).start()
        return 0

    lax.fori_loop(1, chips, send_3, 0)
    buf3[chip] = sol[:, my_rows(0), :]

    def wait_3(k, _):
        j = lax.rem(chip + k, chips)
        remote(sol.at[:, pl.ds(0, piece), :], buf3.at[j], s3.at[0], r3.at[j], (me, slab)).wait_recv()
        return 0

    lax.fori_loop(1, chips, wait_3, 0)

    def back(t, _):
        at = pl.ds(pl.multiple_of(t * 16, 16), 16)
        pairs = [(buf3[j, 0, at, :].astype(f32), buf3[j, 1, at, :].astype(f32)) for j in range(chips)]
        for n, value in enumerate(inverse_transform(pairs)):
            corr[n, at, :] = value.astype(bf16)
        return 0

    lax.fori_loop(0, piece // 16, back, 0)
    here = pl.ds(pl.multiple_of(mine * piece, 16), piece)

    def send_4(k, _):
        n = lax.rem(me + k, members)
        remote(corr.at[n], buf4.at[here, :], s4.at[n], r4.at[mine], (n, slab)).start()
        return 0

    lax.fori_loop(1, members, send_4, 0)
    buf4[here, :] = corr[me]

    def wait_4(i, _):
        @pl.when(i != mine)
        def _():
            remote(corr.at[0], buf4.at[pl.ds(pl.multiple_of(i * piece, 16), piece), :],
                   s4.at[0], r4.at[i], (me, slab)).wait_recv()
        return 0

    lax.fori_loop(0, members, wait_4, 0)

    def finish(p, _):
        for r, n in chunks:
            at = pl.ds(pl.multiple_of(p * rows, 16) + r, n)
            out[at, :] = (state[at, :].astype(f32) + buf4[at, :].astype(f32)).astype(bf16)
        return 0

    lax.fori_loop(0, width, finish, 0)

    @pl.when(me < members - 1)
    def _():
        prev_copy().wait_send()

    for side in range(2):
        @pl.when(sends[side])
        def _():
            halo_copy(side).wait_send()
    for m, (step, first, count, place) in enumerate(moves):
        @pl.when(there(step))
        def _():
            for a in range(3):
                coef_copy(m, a).wait_send()
            target_copy(m).wait_send()

    def drain_members(n, _):
        owner, copy = piece_copy(n)

        @pl.when(owner != me)
        def _():
            copy.wait_send()

        @pl.when(n != me)
        def _():
            remote(corr.at[n], buf4.at[here, :], s4.at[n], r4.at[mine], (n, slab)).wait_send()
        return 0

    lax.fori_loop(0, members, drain_members, 0)

    def drain_chips(k, _):
        j = lax.rem(chip + k, chips)
        spec_copy(j).wait_send()
        remote(sol.at[:, pl.ds(pl.multiple_of(j * piece, 16), piece), :], buf3.at[chip],
               s3.at[j], r3.at[chip], (2 * j + core, slab)).wait_send()
        return 0

    lax.fori_loop(1, chips, drain_chips, 0)


def on_device(state, initial, forcing, kappa, reaction):
    steps, width, rows, depth = state.shape
    assert steps == 1
    members = lax.axis_size("tm")
    slabs = lax.axis_size("space")
    chips = members // 2
    half = width // 2
    total = width * rows
    piece = half * rows // chips
    ext = half + 2 * REACH
    dma = pltpu.SemaphoreType.DMA
    flat = lambda a: a.reshape(total, depth)
    padded = pltpu.VMEM((ext, rows + 16, depth), f32)
    wide = pltpu.VMEM((ext * rows, depth), f32)
    out = pl.pallas_call(
        functools.partial(kernel, members, slabs, width, rows),
        out_shape=jax.ShapeDtypeStruct((total, depth), bf16),
        in_specs=[pl.BlockSpec(memory_space=pltpu.VMEM)] * 5,
        out_specs=pl.BlockSpec(memory_space=pltpu.VMEM),
        scratch_shapes=[
            pltpu.VMEM((total, depth), bf16),
            pltpu.VMEM((2, 2 * rows, depth), bf16),
            pltpu.VMEM((3, ext * rows, depth), bf16),
            pltpu.VMEM((total, depth), bf16),
            pltpu.VMEM((members, piece, depth), bf16),
            pltpu.VMEM((chips, 2, piece, depth), bf16),
            pltpu.VMEM((2, ext * rows, depth), bf16),
            pltpu.VMEM((2, half * rows, depth), bf16),
            pltpu.VMEM((chips, 2, piece, depth), bf16),
            pltpu.VMEM((members, piece, depth), bf16),
            pltpu.VMEM((total, depth), bf16),
            wide, wide, wide, wide, wide,
            padded, padded, padded, padded,
            dma, dma, dma((2,)), dma((2,)), dma((4, 3)), dma((4, 3)),
            dma((members,)), dma((members,)), dma((chips,)), dma((chips,)),
            dma((4,)), dma((4,)), dma((chips,)), dma((chips,)), dma((members,)), dma((members,)),
        ],
        compiler_params=pltpu.CompilerParams(
            collective_id=0, has_side_effects=True, vmem_limit_bytes=40 * 2**20
        ),
    )(flat(state), flat(initial), flat(forcing), flat(kappa), flat(reaction))
    return out.reshape(state.shape)


def solution(mesh):
    cells = P("space", None, None)
    return jax.shard_map(
        on_device,
        mesh=mesh,
        in_specs=(P("tm", "space", None, None), cells, P("tm", "space", None, None), cells, cells),
        out_specs=P("tm", "space", None, None),
        check_vma=False,
    )
```

time: 238 us -> 70 us (0.29)
  other arithmetic: 64.9 us -> 0 us
  Pallas kernels: 0 us -> 64.3 us
  waiting for transfers between devices: 61.1 us -> 0 us
  local copies, waits for them, and re-layouts: 54.5 us -> 5.45 us
  starting transfers between devices: 40.1 us -> 0 us
  blocking collectives: 13.9 us -> 0 us
    pallas_call x0 -> x1, Pallas kernels: none -> 64.3 us  [on_device(): pl.pallas_call(functools.partial(kernel, members, slabs, width, rows), ou...]
    unnamed x1 -> x0, other arithmetic: 45.2 us -> none
    all_to_all x3 -> x0, waiting for transfers between devices: 38.4 us -> none  [the longest x1 14.5 us: on_device(): lax.all_to_all(solved, 'tm', split_axis=3, concat_axis=1, tiled=True)]
    ppermute x11 -> x0, starting transfers between devices: 25.7 us -> none  [the longest x5 16.7 us: with_halo(): lax.ppermute(lax.slice_in_dim(block, block.shape[dim] - width, None, axis...]
    ppermute x11 -> x0, waiting for transfers between devices: 22.7 us -> none  [the longest x5 17.1 us: with_halo(): lax.ppermute(lax.slice_in_dim(block, 0, width, axis=dim), axis, backward)]
    unnamed x19 -> x11, local copies, waits for them, and re-layouts: 22.2 us -> 5.45 us
    all_to_all x3 -> x0, starting transfers between devices: 14.4 us -> none  [the longest x1 6.08 us: on_device(): lax.all_to_all(residual, 'tm', split_axis=2, concat_axis=0, tiled=True)]
    all_to_all x1 -> x0, blocking collectives: 13.9 us -> none  [on_device(): lax.all_to_all(correction, 'tm', split_axis=0, concat_axis=2, tiled=True)]
  transfers between devices with their start and end apart: 14 -> 0, of which waited for: 12 -> 0; matrix products, arithmetic and copies ran while one was open for 1% -> 0% of each run, Pallas kernels for 0% -> 0%
where the time goes in v1:
time: 70 us; the launch traced here: 69.8 us
  Pallas kernels  64.3 us (92%)
  local copies, waits for them, and re-layouts  5.45 us (8%)
    pallas_call x1, Pallas kernels, on_device(): pl.pallas_call(functools.partial(kernel, members, slabs, width, rows), ou...  64.3 us
    unnamed x11, local copies, waits for them, and re-layouts  5.45 us

profile of v1, /device:TPU:0, one launch (start us, length us, event | category | flops | bytes accessed | tf_op | source)
XLA Modules:
  0.0 69.8 jit_solution(16946491192748520996)
XLA Ops:
  0.0 0.0 copy-start
  0.0 0.9 %copy-done = bf16[1,16,64,128]{3,2,1,0:T(8,128)(2,1)S(1)} copy-done((bf16[1,16,64,128]{3,2,1,0:T(8,128)(2,1)S(1)}, bf16[1,16,64,128]{3,2,1,0:T(8,128)(2,1)}, u32[]{:S(2)}) %copy-start) | copy-done | bytes 262168
  1.0 0.0 copy-start.1
  1.0 0.9 %copy-done.1 = bf16[16,64,128]{2,1,0:T(8,128)(2,1)S(1)} copy-done((bf16[16,64,128]{2,1,0:T(8,128)(2,1)S(1)}, bf16[16,64,128]{2,1,0:T(8,128)(2,1)}, u32[]{:S(2)}) %copy-start.1) | copy-done | bytes 262168
  1.9 0.0 copy-start.2
  1.9 0.9 %copy-done.2 = bf16[1,16,64,128]{3,2,1,0:T(8,128)(2,1)S(1)} copy-done((bf16[1,16,64,128]{3,2,1,0:T(8,128)(2,1)S(1)}, bf16[1,16,64,128]{3,2,1,0:T(8,128)(2,1)}, u32[]{:S(2)}) %copy-start.2) | copy-done | bytes 262168
  2.9 0.0 copy-start.3
  2.9 0.9 %copy-done.3 = bf16[16,64,128]{2,1,0:T(8,128)(2,1)S(1)} copy-done((bf16[16,64,128]{2,1,0:T(8,128)(2,1)S(1)}, bf16[16,64,128]{2,1,0:T(8,128)(2,1)}, u32[]{:S(2)}) %copy-start.3) | copy-done | bytes 262168
  3.8 0.0 copy-start.4
  3.8 0.9 %copy-done.4 = bf16[16,64,128]{2,1,0:T(8,128)(2,1)S(1)} copy-done((bf16[16,64,128]{2,1,0:T(8,128)(2,1)S(1)}, bf16[16,64,128]{2,1,0:T(8,128)(2,1)}, u32[]{:S(2)}) %copy-start.4) | copy-done | bytes 262168
  4.8 64.3 %shard_map.55 = bf16[1024,128]{1,0:T(8,128)(2,1)S(1)} custom-call(bf16[1024,128]{1,0:T(8,128)(2,1)S(1)} %bitcast.7, bf16[1024,128]{1,0:T(8,128)(2,1)S(1)} %bitcast.8, bf16[1024,128]{1,0:T(8,128)(2,1)S(1)} %bitcast.9, bf16[1024,128]{1,0:T(8,128)(2,1)S(1)} %bitcast.10, bf16[1024,128]{1,0:T(8,128)(2,1)S(1)} %bitcast.11), custom_call_target="tpu_custom_call" | custom-call | tf_op jit(solution)/shard_map/pallas_call | solution.py:544
  69.1 0.7 %copy.7 = bf16[1,16,64,128]{3,2,1,0:T(8,128)(2,1)} copy(bf16[1,16,64,128]{3,2,1,0:T(8,128)(2,1)S(1)} %bitcast.6) | data formatting | bytes 524288
Async XLA Ops:
  0.0 0.9 %copy-start = (bf16[1,16,64,128]{3,2,1,0:T(8,128)(2,1)S(1)}, bf16[1,16,64,128]{3,2,1,0:T(8,128)(2,1)}, u32[]{:S(2)}) copy-start(bf16[1,16,64,128]{3,2,1,0:T(8,128)(2,1)} %param.5) | copy-start | bytes 786436
  1.0 0.9 %copy-start.1 = (bf16[16,64,128]{2,1,0:T(8,128)(2,1)S(1)}, bf16[16,64,128]{2,1,0:T(8,128)(2,1)}, u32[]{:S(2)}) copy-start(bf16[16,64,128]{2,1,0:T(8,128)(2,1)} %param.6) | copy-start | bytes 786436
  1.9 0.9 %copy-start.2 = (bf16[1,16,64,128]{3,2,1,0:T(8,128)(2,1)S(1)}, bf16[1,16,64,128]{3,2,1,0:T(8,128)(2,1)}, u32[]{:S(2)}) copy-start(bf16[1,16,64,128]{3,2,1,0:T(8,128)(2,1)} %param.7) | copy-start | bytes 786436
  2.9 0.9 %copy-start.3 = (bf16[16,64,128]{2,1,0:T(8,128)(2,1)S(1)}, bf16[16,64,128]{2,1,0:T(8,128)(2,1)}, u32[]{:S(2)}) copy-start(bf16[16,64,128]{2,1,0:T(8,128)(2,1)} %param.8) | copy-start | bytes 786436
  3.8 0.9 %copy-start.4 = (bf16[16,64,128]{2,1,0:T(8,128)(2,1)S(1)}, bf16[16,64,128]{2,1,0:T(8,128)(2,1)}, u32[]{:S(2)}) copy-start(bf16[16,64,128]{2,1,0:T(8,128)(2,1)} %param.9) | copy-start | bytes 786436

commit v2 on v1

--- a/solution.py
+++ b/solution.py
@@ -132,7 +132,8 @@
 
 def kernel(
     members, slabs, width, rows,
-    state, initial, forcing, kappa, reaction, out,
+    state_h, initial_h, forcing_h, kappa_h, reaction_h, out,
+    state, initial, forcing, kappa, reaction, load_s,
     prev, halo, cext, res, buf1, spec, tgt, sol, buf3, corr, buf4,
     ca, cc, ci, x0r, x0i, ar, ai, br, bi,
     prev_s, prev_r, halo_s, halo_r, coef_s, coef_r, s1, r1, s2, r2, sg, rg, s3, r3, s4, r4,
@@ -152,6 +153,16 @@
     parts = 2 * slabs
     chunks = [(r, 16) for r in range(0, rows, 16)]
 
+    loads = [
+        pltpu.make_async_copy(src, dst, load_s.at[k])
+        for k, (src, dst) in enumerate((
+            (state_h, state), (kappa_h, kappa), (reaction_h, reaction),
+            (initial_h, initial), (forcing_h, forcing),
+        ))
+    ]
+    for load in loads:
+        load.start()
+
     barrier = pltpu.get_barrier_semaphore()
 
     def greet(k, _):
@@ -169,6 +180,15 @@
                 pl.semaphore_signal(
                     barrier, inc=1, device_id=(chip * 2 + c, slab + step), device_id_type=MESH
                 )
+    pad = jnp.zeros((8, depth), f32)
+
+    def clear(p, _):
+        for ref in (ar, ai, br, bi):
+            ref[p, 0:8, :] = pad
+            ref[p, 8 + rows : 16 + rows, :] = pad
+        return 0
+
+    lax.fori_loop(0, ext, clear, 0)
     pl.semaphore_wait(
         barrier,
         members - 1 + 2 * has_low.astype(jnp.int32) + 2 * has_high.astype(jnp.int32),
@@ -182,6 +202,8 @@
 
     def prev_copy():
         return remote(state, prev, prev_s, prev_r, (lax.rem(me + 1, members), slab))
+
+    loads[0].wait()
 
     @pl.when(me < members - 1)
     def _():
@@ -225,12 +247,8 @@
         return remote(src, cext.at[a, pl.ds(place * rows, count * rows), :],
                       coef_s.at[m, a], coef_r.at[m, a], device_at(step))
 
-    def target_copy(m):
-        step, first, count, place = moves[m]
-        return remote(tgt.at[:, pl.ds((REACH + first) * rows, count * rows), :],
-                      tgt.at[:, pl.ds(place * rows, count * rows), :],
-                      sg.at[m], rg.at[m], device_at(step))
-
+    for load in loads[1:4]:
+        load.wait()
     for m, (step, first, count, place) in enumerate(moves):
         @pl.when(there(step))
         def _():
@@ -247,15 +265,6 @@
     for a in range(3):
         cext[a, pl.ds(REACH * rows, hr), :] = coefs[a][pl.ds(pl.multiple_of(core * hr, 16), hr), :]
 
-    pad = jnp.zeros((8, depth), f32)
-
-    def clear(p, _):
-        for ref in (ar, ai, br, bi):
-            ref[p, 0:8, :] = pad
-            ref[p, 8 + rows : 16 + rows, :] = pad
-        return 0
-
-    lax.fori_loop(0, ext, clear, 0)
     lane = lax.broadcasted_iota(jnp.int32, (16, depth), 1)
 
     def widen(p, _):
@@ -272,6 +281,8 @@
         for p in range(2):
             at = p if side == 0 else width + 2 + p
             ar[at, 8 : 8 + rows, :] = halo[side, p * rows : (p + 1) * rows, :].astype(f32)
+
+    loads[4].wait()
 
     @pl.when(me == 0)
     def _():
@@ -313,6 +324,76 @@
     mine = core * chips + chip
     buf1[me] = res[pl.ds(pl.multiple_of(mine * piece, 16), piece), :]
 
+    def wait_1(n, _):
+        @pl.when(n != me)
+        def _():
+            remote(res.at[pl.ds(0, piece), :], buf1.at[n], s1.at[0], r1.at[n], (me, slab)).wait_recv()
+        return 0
+
+    lax.fori_loop(0, members, wait_1, 0)
+
+    def transform(t, _):
+        at = pl.ds(pl.multiple_of(t * 16, 16), 16)
+        pairs = forward_transform([buf1[n, at, :].astype(f32) for n in range(members)])
+        for j in range(chips):
+            spec[j, 0, at, :] = pairs[j][0].astype(bf16)
+            spec[j, 1, at, :] = pairs[j][1].astype(bf16)
+        return 0
+
+    lax.fori_loop(0, piece // 16, transform, 0)
+
+    def my_rows(first):
+        return pl.ds(pl.multiple_of(first * rows + chip * piece, 16), piece)
+
+    def spec_copy(j):
+        return remote(spec.at[j], tgt.at[:, my_rows(REACH), :], s2.at[j], r2.at[chip],
+                      (2 * j + core, slab))
+
+    def send_2(k, _):
+        spec_copy(lax.rem(chip + k, chips)).start()
+        return 0
+
+    lax.fori_loop(1, chips, send_2, 0)
+    tgt[:, my_rows(REACH), :] = spec[chip]
+
+    def forward(j, action):
+        at = j * piece
+        for m, (step, first, count, place) in enumerate(moves):
+            inside = jnp.logical_and(at >= first * rows, at < (first + count) * rows)
+
+            @pl.when(jnp.logical_and(there(step), inside))
+            def _():
+                target = pl.multiple_of(place * rows + at - first * rows, 16)
+                copy = remote(
+                    tgt.at[:, pl.ds(pl.multiple_of(REACH * rows + at, 16), piece), :],
+                    tgt.at[:, pl.ds(target, piece), :],
+                    sg.at[m, j], rg.at[m, j], device_at(step))
+                action(copy)
+
+    def arrived(m, j):
+        step, first, count, place = moves[m]
+        at = j * piece
+        inside = jnp.logical_and(at >= first * rows, at < (first + count) * rows)
+
+        @pl.when(jnp.logical_and(there(-step), inside))
+        def _():
+            target = pl.multiple_of(place * rows + at - first * rows, 16)
+            remote(
+                tgt.at[:, pl.ds(REACH * rows, piece), :],
+                tgt.at[:, pl.ds(target, piece), :],
+                sg.at[m, j], rg.at[m, j], (me, slab)).wait_recv()
+
+    forward(chip, lambda copy: copy.start())
+
+    def wait_2(k, _):
+        j = lax.rem(chip + chips - k, chips)
+        remote(spec.at[0], tgt.at[:, pl.ds(pl.multiple_of(REACH * rows + j * piece, 16), piece), :],
+               s2.at[0], r2.at[j], (me, slab)).wait_recv()
+        forward(j, lambda copy: copy.start())
+        return 0
+
+    lax.fori_loop(1, chips, wait_2, 0)
+
     for m, (step, first, count, place) in enumerate(moves):
         @pl.when(there(-step))
         def _():
@@ -341,50 +422,6 @@
         return 0
 
     lax.fori_loop(0, ext, coefficients, 0)
-
-    def wait_1(n, _):
-        @pl.when(n != me)
-        def _():
-            remote(res.at[pl.ds(0, piece), :], buf1.at[n], s1.at[0], r1.at[n], (me, slab)).wait_recv()
-        return 0
-
-    lax.fori_loop(0, members, wait_1, 0)
-
-    def transform(t, _):
-        at = pl.ds(pl.multiple_of(t * 16, 16), 16)
-        pairs = forward_transform([buf1[n, at, :].astype(f32) for n in range(members)])
-        for j in range(chips):
-            spec[j, 0, at, :] = pairs[j][0].astype(bf16)
-            spec[j, 1, at, :] = pairs[j][1].astype(bf16)
-        return 0
-
-    lax.fori_loop(0, piece // 16, transform, 0)
-
-    def my_rows(first):
-        return pl.ds(pl.multiple_of(first * rows + chip * piece, 16), piece)
-
-    def spec_copy(j):
-        return remote(spec.at[j], tgt.at[:, my_rows(REACH), :], s2.at[j], r2.at[chip],
-                      (2 * j + core, slab))
-
-    def send_2(k, _):
-        spec_copy(lax.rem(chip + k, chips)).start()
-        return 0
-
-    lax.fori_loop(1, chips, send_2, 0)
-    tgt[:, my_rows(REACH), :] = spec[chip]
-
-    def wait_2(k, _):
-        j = lax.rem(chip + k, chips)
-        remote(spec.at[0], tgt.at[:, pl.ds(pl.multiple_of(REACH * rows + j * piece, 16), piece), :],
-               s2.at[0], r2.at[j], (me, slab)).wait_recv()
-        return 0
-
-    lax.fori_loop(1, chips, wait_2, 0)
-    for m, (step, first, count, place) in enumerate(moves):
-        @pl.when(there(step))
-        def _():
-            target_copy(m).start()
 
     def opening(p, _):
         for r, n in chunks:
@@ -405,12 +442,19 @@
         return 0
 
     lax.fori_loop(REACH, REACH + half, opening, 0)
-    for m, (step, first, count, place) in enumerate(moves):
-        @pl.when(there(-step))
-        def _():
-            target_copy(m).wait_recv()
+    def arrivals(k, _):
+        j = lax.rem(chip + chips - k, chips)
+        for m in range(4):
+            arrived(m, j)
+        return 0
+
+    lax.fori_loop(0, chips, arrivals, 0)
     lax.fori_loop(0, REACH, opening, 0)
     lax.fori_loop(REACH + half, ext, opening, 0)
+
+    def solved_copy(j):
+        return remote(sol.at[:, pl.ds(pl.multiple_of(j * piece, 16), piece), :], buf3.at[chip],
+                      s3.at[j], r3.at[chip], (2 * j + core, slab))
 
     weights = sweep_weights()
     for k in range(SWEEPS):
@@ -418,7 +462,11 @@
         w = weights[k]
         last = k == SWEEPS - 1
 
-        def sweep(p, _):
+        def sweep(turn, _):
+            p = turn
+            if last:
+                plane = lax.rem(turn - REACH + lax.div(chip, per_plane) + 1, half)
+                p = plane + REACH
             for r, n in chunks:
                 at = pl.ds(pl.multiple_of(p * rows, 16) + r, n)
                 xr, tr = neighbour_sum(sr, p, 8 + r, n, lane)
@@ -433,17 +481,17 @@
                 else:
                     dr[p, 8 + r : 8 + r + n, :] = nr
                     di[p, 8 + r : 8 + r + n, :] = ni
+            if last:
+                for sub in range(per_plane):
+                    j = plane * per_plane + sub
+
+                    @pl.when(j != chip)
+                    def _():
+                        solved_copy(j).start()
             return 0
 
         lax.fori_loop(2 * k + 2, ext - 2 * k - 2, sweep, 0)
 
-    def send_3(k, _):
-        j = lax.rem(chip + k, chips)
-        remote(sol.at[:, pl.ds(pl.multiple_of(j * piece, 16), piece), :], buf3.at[chip],
-               s3.at[j], r3.at[chip], (2 * j + core, slab)).start()
-        return 0
-
-    lax.fori_loop(1, chips, send_3, 0)
     buf3[chip] = sol[:, my_rows(0), :]
 
     def wait_3(k, _):
@@ -501,7 +549,6 @@
         def _():
             for a in range(3):
                 coef_copy(m, a).wait_send()
-            target_copy(m).wait_send()
 
     def drain_members(n, _):
         owner, copy = piece_copy(n)
@@ -520,10 +567,11 @@
     def drain_chips(k, _):
         j = lax.rem(chip + k, chips)
         spec_copy(j).wait_send()
-        remote(sol.at[:, pl.ds(pl.multiple_of(j * piece, 16), piece), :], buf3.at[chip],
-               s3.at[j], r3.at[chip], (2 * j + core, slab)).wait_send()
-        return 0
-
+        forward(j, lambda copy: copy.wait_send())
+        solved_copy(j).wait_send()
+        return 0
+
+    forward(chip, lambda copy: copy.wait_send())
     lax.fori_loop(1, chips, drain_chips, 0)
 
 
@@ -544,9 +592,10 @@
     out = pl.pallas_call(
         functools.partial(kernel, members, slabs, width, rows),
         out_shape=jax.ShapeDtypeStruct((total, depth), bf16),
-        in_specs=[pl.BlockSpec(memory_space=pltpu.VMEM)] * 5,
+        in_specs=[pl.BlockSpec(memory_space=pltpu.HBM)] * 5,
         out_specs=pl.BlockSpec(memory_space=pltpu.VMEM),
         scratch_shapes=[
+            *[pltpu.VMEM((total, depth), bf16)] * 5, dma((5,)),
             pltpu.VMEM((total, depth), bf16),
             pltpu.VMEM((2, 2 * rows, depth), bf16),
             pltpu.VMEM((3, ext * rows, depth), bf16),
@@ -562,7 +611,7 @@
             padded, padded, padded, padded,
             dma, dma, dma((2,)), dma((2,)), dma((4, 3)), dma((4, 3)),
             dma((members,)), dma((members,)), dma((chips,)), dma((chips,)),
-            dma((4,)), dma((4,)), dma((chips,)), dma((chips,)), dma((members,)), dma((members,)),
+            dma((4, chips)), dma((4, chips)), dma((chips,)), dma((chips,)), dma((members,)), dma((members,)),
         ],
         compiler_params=pltpu.CompilerParams(
             collective_id=0, has_side_effects=True, vmem_limit_bytes=40 * 2**20

time: 70 us -> 66.2 us (0.946)
  Pallas kernels: 64.3 us -> 60.4 us
    pallas_call x1, Pallas kernels: 64.3 us -> 60.4 us  [on_device(): pl.pallas_call(functools.partial(kernel, members, slabs, width, rows), ou...]
where the time goes in v2:
time: 66.2 us; the launch traced here: 65.9 us
  Pallas kernels  60.4 us (91%)
  local copies, waits for them, and re-layouts  5.45 us (8%)
    pallas_call x1, Pallas kernels, on_device(): pl.pallas_call(functools.partial(kernel, members, slabs, width, rows), ou...  60.4 us
    unnamed x11, local copies, waits for them, and re-layouts  5.45 us

profile of v2, /device:TPU:0, one launch (start us, length us, event | category | flops | bytes accessed | tf_op | source)
XLA Modules:
  0.0 65.9 jit_solution(18030462741224112027)
XLA Ops:
  0.0 0.0 copy-start
  0.0 0.9 %copy-done = bf16[1,16,64,128]{3,2,1,0:T(8,128)(2,1)S(1)} copy-done((bf16[1,16,64,128]{3,2,1,0:T(8,128)(2,1)S(1)}, bf16[1,16,64,128]{3,2,1,0:T(8,128)(2,1)}, u32[]{:S(2)}) %copy-start) | copy-done | bytes 262168
  1.0 0.0 copy-start.1
  1.0 0.9 %copy-done.1 = bf16[16,64,128]{2,1,0:T(8,128)(2,1)S(1)} copy-done((bf16[16,64,128]{2,1,0:T(8,128)(2,1)S(1)}, bf16[16,64,128]{2,1,0:T(8,128)(2,1)}, u32[]{:S(2)}) %copy-start.1) | copy-done | bytes 262168
  1.9 0.0 copy-start.2
  1.9 0.9 %copy-done.2 = bf16[1,16,64,128]{3,2,1,0:T(8,128)(2,1)S(1)} copy-done((bf16[1,16,64,128]{3,2,1,0:T(8,128)(2,1)S(1)}, bf16[1,16,64,128]{3,2,1,0:T(8,128)(2,1)}, u32[]{:S(2)}) %copy-start.2) | copy-done | bytes 262168
  2.9 0.0 copy-start.3
  2.9 0.9 %copy-done.3 = bf16[16,64,128]{2,1,0:T(8,128)(2,1)S(1)} copy-done((bf16[16,64,128]{2,1,0:T(8,128)(2,1)S(1)}, bf16[16,64,128]{2,1,0:T(8,128)(2,1)}, u32[]{:S(2)}) %copy-start.3) | copy-done | bytes 262168
  3.8 0.0 copy-start.4
  3.8 0.9 %copy-done.4 = bf16[16,64,128]{2,1,0:T(8,128)(2,1)S(1)} copy-done((bf16[16,64,128]{2,1,0:T(8,128)(2,1)S(1)}, bf16[16,64,128]{2,1,0:T(8,128)(2,1)}, u32[]{:S(2)}) %copy-start.4) | copy-done | bytes 262168
  4.8 60.4 %shard_map.55 = bf16[1024,128]{1,0:T(8,128)(2,1)S(1)} custom-call(bf16[1024,128]{1,0:T(8,128)(2,1)S(1)} %bitcast.7, bf16[1024,128]{1,0:T(8,128)(2,1)S(1)} %bitcast.8, bf16[1024,128]{1,0:T(8,128)(2,1)S(1)} %bitcast.9, bf16[1024,128]{1,0:T(8,128)(2,1)S(1)} %bitcast.10, bf16[1024,128]{1,0:T(8,128)(2,1)S(1)} %bitcast.11), custom_call_target="tpu_custom_call" | custom-call | tf_op jit(solution)/shard_map/pallas_call | solution.py:592
  65.2 0.7 %copy.7 = bf16[1,16,64,128]{3,2,1,0:T(8,128)(2,1)} copy(bf16[1,16,64,128]{3,2,1,0:T(8,128)(2,1)S(1)} %bitcast.6) | data formatting | bytes 524288
Async XLA Ops:
  0.0 0.9 %copy-start = (bf16[1,16,64,128]{3,2,1,0:T(8,128)(2,1)S(1)}, bf16[1,16,64,128]{3,2,1,0:T(8,128)(2,1)}, u32[]{:S(2)}) copy-start(bf16[1,16,64,128]{3,2,1,0:T(8,128)(2,1)} %param.5) | copy-start | bytes 786436
  1.0 0.9 %copy-start.1 = (bf16[16,64,128]{2,1,0:T(8,128)(2,1)S(1)}, bf16[16,64,128]{2,1,0:T(8,128)(2,1)}, u32[]{:S(2)}) copy-start(bf16[16,64,128]{2,1,0:T(8,128)(2,1)} %param.6) | copy-start | bytes 786436
  1.9 0.9 %copy-start.2 = (bf16[1,16,64,128]{3,2,1,0:T(8,128)(2,1)S(1)}, bf16[1,16,64,128]{3,2,1,0:T(8,128)(2,1)}, u32[]{:S(2)}) copy-start(bf16[1,16,64,128]{3,2,1,0:T(8,128)(2,1)} %param.7) | copy-start | bytes 786436
  2.9 0.9 %copy-start.3 = (bf16[16,64,128]{2,1,0:T(8,128)(2,1)S(1)}, bf16[16,64,128]{2,1,0:T(8,128)(2,1)}, u32[]{:S(2)}) copy-start(bf16[16,64,128]{2,1,0:T(8,128)(2,1)} %param.8) | copy-start | bytes 786436
  3.8 0.9 %copy-start.4 = (bf16[16,64,128]{2,1,0:T(8,128)(2,1)S(1)}, bf16[16,64,128]{2,1,0:T(8,128)(2,1)}, u32[]{:S(2)}) copy-start(bf16[16,64,128]{2,1,0:T(8,128)(2,1)} %param.9) | copy-start | bytes 786436

commit v3 on v2

--- a/solution.py
+++ b/solution.py
@@ -130,12 +130,34 @@
     return c, near * 0.5 + far
 
 
+def around(ref, p, t, along):
+    near = (ref[p - 1, t] + ref[p + 1, t]) + (ref[p, t - 1] + ref[p, t + 1])
+    far = (ref[p - 2, t] + ref[p + 2, t]) + (ref[p, t - 2] + ref[p, t + 2])
+    return ref[p, t], near * 0.5 + far + along
+
+
+def split(x):
+    high = x.astype(bf16)
+    rest = x - high.astype(f32)
+    mid = rest.astype(bf16)
+    low = (rest - mid.astype(f32)).astype(bf16)
+    return jnp.concatenate([high, mid, low], axis=1)
+
+
+def put(ref, p, y, tiles, value, row):
+    ref[p, y + 2] = value
+    if y < 2:
+        ref[p, y + 2 + tiles] = jnp.where(row < 7, pltpu.roll(value, 7, 0), jnp.zeros_like(value))
+    if y >= tiles - 2:
+        ref[p, y + 2 - tiles] = jnp.where(row >= 1, pltpu.roll(value, 1, 0), jnp.zeros_like(value))
+
+
 def kernel(
     members, slabs, width, rows,
     state_h, initial_h, forcing_h, kappa_h, reaction_h, out,
     state, initial, forcing, kappa, reaction, load_s,
     prev, halo, cext, res, buf1, spec, tgt, sol, buf3, corr, buf4,
-    ca, cc, ci, x0r, x0i, ar, ai, br, bi,
+    ca, cc, ci, x0r, x0i, kp, pad_s, band, ar, ai, br, bi,
     prev_s, prev_r, halo_s, halo_r, coef_s, coef_r, s1, r1, s2, r2, sg, rg, s3, r3, s4, r4,
 ):
     chips = members // 2
@@ -183,12 +205,11 @@
     pad = jnp.zeros((8, depth), f32)
 
     def clear(p, _):
-        for ref in (ar, ai, br, bi):
-            ref[p, 0:8, :] = pad
-            ref[p, 8 + rows : 16 + rows, :] = pad
-        return 0
-
-    lax.fori_loop(0, ext, clear, 0)
+        pad_s[p, 0:8, :] = pad
+        pad_s[p, 8 + rows : 16 + rows, :] = pad
+        return 0
+
+    lax.fori_loop(0, width + 4, clear, 0)
     pl.semaphore_wait(
         barrier,
         members - 1 + 2 * has_low.astype(jnp.int32) + 2 * has_high.astype(jnp.int32),
@@ -266,11 +287,24 @@
         cext[a, pl.ds(REACH * rows, hr), :] = coefs[a][pl.ds(pl.multiple_of(core * hr, 16), hr), :]
 
     lane = lax.broadcasted_iota(jnp.int32, (16, depth), 1)
+    apart = jnp.abs(
+        lax.broadcasted_iota(jnp.int32, (depth, depth), 0)
+        - lax.broadcasted_iota(jnp.int32, (depth, depth), 1)
+    )
+    taps = jnp.where(apart == 1, 0.5, jnp.where(apart == 2, 1.0, 0.0)).astype(bf16)
+    for k in range(3):
+        band[k * depth : (k + 1) * depth, :] = taps
+    row8 = lax.broadcasted_iota(jnp.int32, (8, depth), 0)
+    tiles = rows // 8
+
+    def strided(ref, p, y):
+        first = pl.multiple_of(p * rows, 16)
+        return jnp.concatenate([ref[pl.ds(first + y + d, 8, stride=tiles), :] for d in range(2)], axis=0)
 
     def widen(p, _):
         for r, n in chunks:
             at = pl.ds(pl.multiple_of(p * rows, 16) + r, n)
-            ar[p + 2, 8 + r : 8 + r + n, :] = state[at, :].astype(f32)
+            pad_s[p + 2, 8 + r : 8 + r + n, :] = state[at, :].astype(f32)
         return 0
 
     lax.fori_loop(0, width, widen, 0)
@@ -280,7 +314,7 @@
             halo_copy(side).wait_recv()
         for p in range(2):
             at = p if side == 0 else width + 2 + p
-            ar[at, 8 : 8 + rows, :] = halo[side, p * rows : (p + 1) * rows, :].astype(f32)
+            pad_s[at, 8 : 8 + rows, :] = halo[side, p * rows : (p + 1) * rows, :].astype(f32)
 
     loads[4].wait()
 
@@ -303,14 +337,17 @@
         p = lax.rem(k + core * half + lax.div(chip, per_plane) + 1, width)
         for r, n in chunks:
             at = pl.ds(pl.multiple_of(p * rows, 16) + r, n)
-            c, total = neighbour_sum(ar, p + 2, 8 + r, n, lane)
+            c, total = neighbour_sum(pad_s, p + 2, 8 + r, n, lane)
             kap = kappa[at, :].astype(f32)
             value = (
                 forcing[at, :].astype(f32) - c + prev[at, :].astype(f32)
                 - kap * (9.0 * c - total)
                 - reaction[at, :].astype(f32) * c * c * c
             )
-            res[at, :] = value.astype(bf16)
+            x0r[at, :] = value
+        for y in range(0, tiles, 2):
+            to = pl.ds(pl.multiple_of(p * rows, 16) + 8 * y, 16)
+            res[to, :] = strided(x0r, p, y).astype(bf16)
         for sub in range(per_plane):
             i = p * per_plane + sub
             owner, copy = piece_copy(i)
@@ -411,11 +448,16 @@
             at = pl.ds(pl.multiple_of(p * rows, 16) + r, n)
             kap = cext[0, at, :].astype(f32)
             ini = cext[2, at, :].astype(f32)
-            base = 9.0 * kap + 3.0 * cext[1, at, :].astype(f32) * ini * ini
+            x0r[at, :] = kap
+            x0i[at, :] = 9.0 * kap + 3.0 * cext[1, at, :].astype(f32) * ini * ini
+        for y in range(0, tiles, 2):
+            at = pl.ds(pl.multiple_of(p * rows, 16) + 8 * y, 16)
+            base = strided(x0i, p, y)
             da = shift_a + base
             dc = shift_c + base
             ia = 1.0 / (da * da + shift_i * shift_i)
             ic = 1.0 / (dc * dc + shift_i * shift_i)
+            kp[at, :] = strided(x0r, p, y)
             ca[at, :] = da * ia
             cc[at, :] = dc * ic
             ci[at, :] = shift_i * ia
@@ -428,14 +470,15 @@
             at = pl.ds(pl.multiple_of(p * rows, 16) + r, n)
             yr = tgt[0, at, :].astype(f32)
             yi = tgt[1, at, :].astype(f32)
-            kap = cext[0, at, :].astype(f32)
+            kap = kp[at, :]
             a, c, i = ca[at, :], cc[at, :], ci[at, :]
             xr = yr * a + yi * i
             xi = yi * c - yr * i
             x0r[at, :] = xr
             x0i[at, :] = xi
-            ar[p, 8 + r : 8 + r + n, :] = xr
-            ai[p, 8 + r : 8 + r + n, :] = xi
+            for d in range(2):
+                put(ar, p, r // 8 + d, tiles, xr[8 * d : 8 * d + 8, :], row8)
+                put(ai, p, r // 8 + d, tiles, xi[8 * d : 8 * d + 8, :], row8)
             ca[at, :] = a * kap
             cc[at, :] = c * kap
             ci[at, :] = i * kap
@@ -463,34 +506,46 @@
         last = k == SWEEPS - 1
 
         def sweep(turn, _):
-            p = turn
+            p0 = 2 * k + 2 + 4 * turn
             if last:
-                plane = lax.rem(turn - REACH + lax.div(chip, per_plane) + 1, half)
-                p = plane + REACH
-            for r, n in chunks:
-                at = pl.ds(pl.multiple_of(p * rows, 16) + r, n)
-                xr, tr = neighbour_sum(sr, p, 8 + r, n, lane)
-                xi, ti = neighbour_sum(si, p, 8 + r, n, lane)
-                i = ci[at, :]
-                nr = (x0r[at, :] + ca[at, :] * tr + i * ti) * w + xr * (1.0 - w)
-                ni = (x0i[at, :] + cc[at, :] * ti - i * tr) * w + xi * (1.0 - w)
+                p0 = REACH + lax.rem(4 * turn + 4 * lax.div(lax.div(chip, per_plane) + 1, 4), half)
+            lifted = [
+                ref[p0 + e, 2 : 2 + tiles].reshape(rows, depth) for e in range(4) for ref in (sr, si)
+            ]
+            along = jnp.dot(
+                split(jnp.concatenate(lifted, axis=0)), band[...], preferred_element_type=f32
+            )
+            for e in range(4):
+                p = p0 + e
+                solved = []
+                for y in range(tiles):
+                    at = pl.ds(pl.multiple_of(p * rows, 16) + 8 * y, 8)
+                    first = 2 * e * rows + 8 * y
+                    xr, tr = around(sr, p, y + 2, along[first : first + 8, :])
+                    xi, ti = around(si, p, y + 2, along[first + rows : first + rows + 8, :])
+                    i = ci[at, :]
+                    nr = (x0r[at, :] + ca[at, :] * tr + i * ti) * w + xr * (1.0 - w)
+                    ni = (x0i[at, :] + cc[at, :] * ti - i * tr) * w + xi * (1.0 - w)
+                    if last:
+                        solved.append((nr, ni))
+                        if y % 2:
+                            to = pl.ds(pl.multiple_of((p - REACH) * rows, 16) + 8 * y - 8, 16)
+                            for k2 in range(2):
+                                both = jnp.concatenate([solved[y - 1][k2], solved[y][k2]], axis=0)
+                                sol[k2, to, :] = both.astype(bf16)
+                    else:
+                        put(dr, p, y, tiles, nr, row8)
+                        put(di, p, y, tiles, ni, row8)
                 if last:
-                    to = pl.ds(pl.multiple_of((p - REACH) * rows, 16) + r, n)
-                    sol[0, to, :] = nr.astype(bf16)
-                    sol[1, to, :] = ni.astype(bf16)
-                else:
-                    dr[p, 8 + r : 8 + r + n, :] = nr
-                    di[p, 8 + r : 8 + r + n, :] = ni
-            if last:
-                for sub in range(per_plane):
-                    j = plane * per_plane + sub
-
-                    @pl.when(j != chip)
-                    def _():
-                        solved_copy(j).start()
+                    for sub in range(per_plane):
+                        j = (p - REACH) * per_plane + sub
+
+                        @pl.when(j != chip)
+                        def _():
+                            solved_copy(j).start()
             return 0
 
-        lax.fori_loop(2 * k + 2, ext - 2 * k - 2, sweep, 0)
+        lax.fori_loop(0, (ext - 4 * k - 4) // 4, sweep, 0)
 
     buf3[chip] = sol[:, my_rows(0), :]
 
@@ -529,9 +584,16 @@
     lax.fori_loop(0, members, wait_4, 0)
 
     def finish(p, _):
+        first = pl.multiple_of(p * rows, 16)
         for r, n in chunks:
-            at = pl.ds(pl.multiple_of(p * rows, 16) + r, n)
-            out[at, :] = (state[at, :].astype(f32) + buf4[at, :].astype(f32)).astype(bf16)
+            at = pl.ds(first + r, n)
+            x0r[at, :] = buf4[at, :].astype(f32)
+        for g in range(0, 8, 2):
+            at = pl.ds(first + g * tiles, 2 * tiles)
+            natural = jnp.concatenate(
+                [x0r[pl.ds(first + g + d, tiles, stride=8), :] for d in range(2)], axis=0
+            )
+            out[at, :] = (state[at, :].astype(f32) + natural).astype(bf16)
         return 0
 
     lax.fori_loop(0, width, finish, 0)
@@ -587,7 +649,7 @@
     ext = half + 2 * REACH
     dma = pltpu.SemaphoreType.DMA
     flat = lambda a: a.reshape(total, depth)
-    padded = pltpu.VMEM((ext, rows + 16, depth), f32)
+    padded = pltpu.VMEM((ext, rows // 8 + 4, 8, depth), f32)
     wide = pltpu.VMEM((ext * rows, depth), f32)
     out = pl.pallas_call(
         functools.partial(kernel, members, slabs, width, rows),
@@ -607,7 +669,8 @@
             pltpu.VMEM((chips, 2, piece, depth), bf16),
             pltpu.VMEM((members, piece, depth), bf16),
             pltpu.VMEM((total, depth), bf16),
-            wide, wide, wide, wide, wide,
+            wide, wide, wide, wide, wide, wide,
+            pltpu.VMEM((width + 4, rows + 16, depth), f32), pltpu.VMEM((3 * depth, depth), bf16),
             padded, padded, padded, padded,
             dma, dma, dma((2,)), dma((2,)), dma((4, 3)), dma((4, 3)),
             dma((members,)), dma((members,)), dma((chips,)), dma((chips,)),

time: 66.2 us -> 59.1 us (0.89)
  Pallas kernels: 60.4 us -> 52.8 us
    pallas_call x1, Pallas kernels: 60.4 us -> 52.8 us  [on_device(): pl.pallas_call(functools.partial(kernel, members, slabs, width, rows), ou...]
where the time goes in v3:
time: 59.1 us; the launch traced here: 58.3 us
  Pallas kernels  52.8 us (89%)
  local copies, waits for them, and re-layouts  5.45 us (9%)
    pallas_call x1, Pallas kernels, on_device(): pl.pallas_call(functools.partial(kernel, members, slabs, width, rows), ou...  52.8 us
    unnamed x11, local copies, waits for them, and re-layouts  5.45 us

profile of v3, /device:TPU:0, one launch (start us, length us, event | category | flops | bytes accessed | tf_op | source)
XLA Modules:
  0.0 58.3 jit_solution(3046799901838209343)
XLA Ops:
  0.0 0.0 copy-start
  0.0 0.9 %copy-done = bf16[1,16,64,128]{3,2,1,0:T(8,128)(2,1)S(1)} copy-done((bf16[1,16,64,128]{3,2,1,0:T(8,128)(2,1)S(1)}, bf16[1,16,64,128]{3,2,1,0:T(8,128)(2,1)}, u32[]{:S(2)}) %copy-start) | copy-done | bytes 262168
  1.0 0.0 copy-start.1
  1.0 0.9 %copy-done.1 = bf16[16,64,128]{2,1,0:T(8,128)(2,1)S(1)} copy-done((bf16[16,64,128]{2,1,0:T(8,128)(2,1)S(1)}, bf16[16,64,128]{2,1,0:T(8,128)(2,1)}, u32[]{:S(2)}) %copy-start.1) | copy-done | bytes 262168
  1.9 0.0 copy-start.2
  1.9 0.9 %copy-done.2 = bf16[1,16,64,128]{3,2,1,0:T(8,128)(2,1)S(1)} copy-done((bf16[1,16,64,128]{3,2,1,0:T(8,128)(2,1)S(1)}, bf16[1,16,64,128]{3,2,1,0:T(8,128)(2,1)}, u32[]{:S(2)}) %copy-start.2) | copy-done | bytes 262168
  2.9 0.0 copy-start.3
  2.9 0.9 %copy-done.3 = bf16[16,64,128]{2,1,0:T(8,128)(2,1)S(1)} copy-done((bf16[16,64,128]{2,1,0:T(8,128)(2,1)S(1)}, bf16[16,64,128]{2,1,0:T(8,128)(2,1)}, u32[]{:S(2)}) %copy-start.3) | copy-done | bytes 262168
  3.8 0.0 copy-start.4
  3.8 0.9 %copy-done.4 = bf16[16,64,128]{2,1,0:T(8,128)(2,1)S(1)} copy-done((bf16[16,64,128]{2,1,0:T(8,128)(2,1)S(1)}, bf16[16,64,128]{2,1,0:T(8,128)(2,1)}, u32[]{:S(2)}) %copy-start.4) | copy-done | bytes 262168
  4.8 52.8 %shard_map.55 = bf16[1024,128]{1,0:T(8,128)(2,1)S(1)} custom-call(bf16[1024,128]{1,0:T(8,128)(2,1)S(1)} %bitcast.7, bf16[1024,128]{1,0:T(8,128)(2,1)S(1)} %bitcast.8, bf16[1024,128]{1,0:T(8,128)(2,1)S(1)} %bitcast.9, bf16[1024,128]{1,0:T(8,128)(2,1)S(1)} %bitcast.10, bf16[1024,128]{1,0:T(8,128)(2,1)S(1)} %bitcast.11), custom_call_target="tpu_custom_call" | custom-call | tf_op jit(solution)/shard_map/pallas_call | solution.py:654
  57.6 0.7 %copy.7 = bf16[1,16,64,128]{3,2,1,0:T(8,128)(2,1)} copy(bf16[1,16,64,128]{3,2,1,0:T(8,128)(2,1)S(1)} %bitcast.6) | data formatting | bytes 524288
Async XLA Ops:
  0.0 0.9 %copy-start = (bf16[1,16,64,128]{3,2,1,0:T(8,128)(2,1)S(1)}, bf16[1,16,64,128]{3,2,1,0:T(8,128)(2,1)}, u32[]{:S(2)}) copy-start(bf16[1,16,64,128]{3,2,1,0:T(8,128)(2,1)} %param.5) | copy-start | bytes 786436
  1.0 0.9 %copy-start.1 = (bf16[16,64,128]{2,1,0:T(8,128)(2,1)S(1)}, bf16[16,64,128]{2,1,0:T(8,128)(2,1)}, u32[]{:S(2)}) copy-start(bf16[16,64,128]{2,1,0:T(8,128)(2,1)} %param.6) | copy-start | bytes 786436
  1.9 0.9 %copy-start.2 = (bf16[1,16,64,128]{3,2,1,0:T(8,128)(2,1)S(1)}, bf16[1,16,64,128]{3,2,1,0:T(8,128)(2,1)}, u32[]{:S(2)}) copy-start(bf16[1,16,64,128]{3,2,1,0:T(8,128)(2,1)} %param.7) | copy-start | bytes 786436
  2.9 0.9 %copy-start.3 = (bf16[16,64,128]{2,1,0:T(8,128)(2,1)S(1)}, bf16[16,64,128]{2,1,0:T(8,128)(2,1)}, u32[]{:S(2)}) copy-start(bf16[16,64,128]{2,1,0:T(8,128)(2,1)} %param.8) | copy-start | bytes 786436
  3.8 0.9 %copy-start.4 = (bf16[16,64,128]{2,1,0:T(8,128)(2,1)S(1)}, bf16[16,64,128]{2,1,0:T(8,128)(2,1)}, u32[]{:S(2)}) copy-start(bf16[16,64,128]{2,1,0:T(8,128)(2,1)} %param.9) | copy-start | bytes 786436
